TPU v7x, 32 devices: a whole 2x2x4 slice. The times are simulated.
32 devices in a mesh: mem: 4 (over y, x), tok: 8 (over z, core).
Axes of the slice: x: 2, y: 2, z: 4, core: 2. Of those that a mesh axis runs over, the one named last changes fastest.
Arguments:
- queries: bfloat16 [8192, 4096], P('tok', 'mem'), may hold values from -6 to 6
- keys: bfloat16 [8192, 4096], P('tok', 'mem'), may hold values from -6 to 6
- values: bfloat16 [8192, 4096], P('tok', 'mem'), may hold values from -6 to 6
- memory: bfloat16 [32, 128, 128, 256], P('mem', 'tok'), may hold values from -6 to 6
- block_ids: int32 [16, 32, 4], P('tok', 'mem'), may hold values from 0 to 127, as said below
- gate_bias: float32 [32], P('mem'), may hold values from -2 to 2
- grad_out: bfloat16 [8192, 4096], P('tok', 'mem'), may hold values from -6 to 6
Outputs:
- output: bfloat16 [8192, 4096], P('tok', 'mem')
- grad_queries: bfloat16 [8192, 4096], P('tok', 'mem')
- grad_keys: bfloat16 [8192, 4096], P('tok', 'mem')
- grad_values: bfloat16 [8192, 4096], P('tok', 'mem')
Inputs may be any that keep to these rules, and one draw needn't show every extreme that they name: `block_ids`: within one span and head the 4 ids differ. The ids held by one device (2 spans, 8 heads) name at most 16 blocks of any one memory shard (id // 16); in every draw some shard is named exactly 16 times by every such device.
All inputs are finite; a program needn't handle non-finite values.
Results may differ from a plain program's by a relative error of at most 0.02.
Values may be sent and summed in bfloat16 or wider, within the bound.
No kernel may reach another device: no remote copies, remote signals or barrier semaphores. Data moves between devices by JAX's collectives and lax.ppermute only.
A program may use at most 128 MiB of HBM per device.

v0:
```python
import jax
import jax.numpy as jnp
from jax import lax
from jax.sharding import PartitionSpec as P

SPAN_TOKENS = 512
BLOCK = 128
R = 4


def passed_along(block, axis, distance):
    devices = range(lax.axis_size(axis))
    route = [(i - distance, i) for i in devices if i - distance in devices]
    return lax.ppermute(block, axis, route)


def head_pass(query, keys_ext, values_ext, mem_keys, mem_values, grad_rows, gate_value, prev_ok):
    length = query.shape[0]
    scaling = query.shape[1] ** (-0.5)
    row_ids = jnp.arange(length)[:, None]
    col_ids = jnp.arange(2 * length)[None, :]
    allowed = (col_ids <= row_ids + length) & ((col_ids >= length) | prev_ok)
    scores = jnp.dot(query, keys_ext.T, preferred_element_type=jnp.float32) * scaling
    scores = jnp.where(allowed, scores, -jnp.inf)
    row_max = jnp.max(scores, axis=1, keepdims=True)
    weights = jnp.where(allowed, jnp.exp(scores - row_max), 0.0)
    row_sum = jnp.sum(weights, axis=1, keepdims=True)
    attention_weights = (weights / row_sum).astype(jnp.bfloat16)
    local_out = jnp.dot(attention_weights, values_ext, preferred_element_type=jnp.float32)
    mem_scores = jnp.dot(query, mem_keys.T, preferred_element_type=jnp.float32) * scaling
    mem_max = jnp.max(mem_scores, axis=1, keepdims=True)
    mem_weights = jnp.exp(mem_scores - mem_max)
    mem_probs = (mem_weights / jnp.sum(mem_weights, axis=1, keepdims=True)).astype(jnp.bfloat16)
    mem_out = jnp.dot(mem_probs, mem_values, preferred_element_type=jnp.float32)
    output = gate_value * mem_out + (1.0 - gate_value) * local_out
    grad_float = grad_rows.astype(jnp.float32)
    local_gradient = ((1.0 - gate_value) * grad_float).astype(jnp.bfloat16)
    grad_mem = (gate_value * grad_float).astype(jnp.bfloat16)
    local_dprobs = jnp.dot(local_gradient, values_ext.T, preferred_element_type=jnp.float32)
    extended_value_gradient = jnp.dot(
        attention_weights.T, local_gradient, preferred_element_type=jnp.float32
    )
    probs_float = attention_weights.astype(jnp.float32)
    row_dot = jnp.sum(probs_float * local_dprobs, axis=1, keepdims=True)
    local_dscores = (probs_float * (local_dprobs - row_dot) * scaling).astype(jnp.bfloat16)
    query_gradient = jnp.dot(local_dscores, keys_ext, preferred_element_type=jnp.float32)
    extended_key_gradient = jnp.dot(local_dscores.T, query, preferred_element_type=jnp.float32)
    mem_dprobs = jnp.dot(grad_mem, mem_values.T, preferred_element_type=jnp.float32)
    mem_float = mem_probs.astype(jnp.float32)
    mem_dot = jnp.sum(mem_float * mem_dprobs, axis=1, keepdims=True)
    mem_dscores = (mem_float * (mem_dprobs - mem_dot) * scaling).astype(jnp.bfloat16)
    query_gradient = query_gradient + jnp.dot(
        mem_dscores, mem_keys, preferred_element_type=jnp.float32
    )
    return (
        output.astype(jnp.bfloat16),
        query_gradient.astype(jnp.bfloat16),
        extended_key_gradient,
        extended_value_gradient,
        row_max[:, 0],
        row_sum[:, 0],
        row_dot[:, 0],
    )


def split_heads(matrix, head_count):
    return matrix.reshape(matrix.shape[0], head_count, -1).transpose(1, 0, 2)


def join_heads(stacked):
    return stacked.transpose(1, 0, 2).reshape(stacked.shape[1], -1)


def span_sweep(query, keys_ext, values_ext, blocks, grad_rows, gates, prev_ok):
    head_count = gates.shape[0]
    head_size = blocks.shape[-1] // 2
    mem_keys = blocks[..., :head_size].reshape(head_count, -1, head_size)
    mem_values = blocks[..., head_size:].reshape(head_count, -1, head_size)

    def per_head(inputs):
        return head_pass(
            inputs[0], inputs[1], inputs[2], inputs[3], inputs[4], inputs[5], inputs[6], prev_ok
        )

    result = lax.map(
        per_head,
        (
            split_heads(query, head_count),
            split_heads(keys_ext, head_count),
            split_heads(values_ext, head_count),
            mem_keys,
            mem_values,
            split_heads(grad_rows, head_count),
            gates,
        ),
    )
    return (
        join_heads(result[0]),
        join_heads(result[1]),
        join_heads(result[2]),
        join_heads(result[3]),
        (result[4], result[5], result[6]),
    )


def per_device(queries, keys, values, memory, block_ids, gate_bias, grad_out):
    tok_count = lax.axis_size("tok")
    my_rank = lax.axis_index("tok")
    heads_here = gate_bias.shape[0]
    span_count = queries.shape[0] // SPAN_TOKENS
    gates = jax.nn.sigmoid(gate_bias)
    tail_rows = jnp.stack([keys[-SPAN_TOKENS:], values[-SPAN_TOKENS:]])
    before = passed_along(tail_rows, "tok", 1)
    keys_ext = jnp.concatenate([before[0], keys], axis=0)
    values_ext = jnp.concatenate([before[1], values], axis=0)
    blocks_here = memory.shape[1]
    wanted = block_ids.reshape(-1)
    request_count = wanted.shape[0]
    owner_rank = wanted // blocks_here
    head_index = jnp.arange(request_count) // R % heads_here
    request_code = head_index * blocks_here + wanted % blocks_here
    order_ids = jnp.arange(request_count)
    same_owner = owner_rank[:, None] == owner_rank[None, :]
    slot_index = jnp.sum(same_owner & (order_ids[None, :] < order_ids[:, None]), axis=1)
    capacity = 2 * request_count // tok_count
    to_owner = (owner_rank[:, None] == jnp.arange(tok_count)[None, :]).astype(jnp.int32)
    to_slot = (slot_index[:, None] == jnp.arange(capacity)[None, :]).astype(jnp.int32)
    request_table = jnp.sum(
        request_code[:, None, None] * to_owner[:, :, None] * to_slot[:, None, :], axis=0
    )
    mem_flat = memory.reshape(-1, BLOCK, memory.shape[-1])
    found = mem_flat[lax.all_to_all(request_table, "tok", split_axis=0, concat_axis=0, tiled=True)]
    returned = lax.all_to_all(found, "tok", split_axis=0, concat_axis=0, tiled=True)
    picked = returned.reshape(-1, BLOCK, memory.shape[-1])[owner_rank * capacity + slot_index]
    picked = picked.reshape(span_count, heads_here, R, BLOCK, memory.shape[-1])
    outputs, grad_qs, own_keys, current_values, lead_keys, preceding_values = (
        [],
        [],
        [],
        [],
        [],
        [],
    )
    for index in range(span_count):
        rows_start = index * SPAN_TOKENS
        prev_ok = (my_rank > 0) | (index > 0)
        output, query_gradient, extended_key_gradient, extended_value_gradient, softmax_totals = (
            span_sweep(
                queries[rows_start : rows_start + SPAN_TOKENS],
                keys_ext[rows_start : rows_start + 2 * SPAN_TOKENS],
                values_ext[rows_start : rows_start + 2 * SPAN_TOKENS],
                picked[index],
                grad_out[rows_start : rows_start + SPAN_TOKENS],
                gates,
                prev_ok,
            )
        )
        outputs.append(output)
        grad_qs.append(query_gradient)
        own_keys.append(extended_key_gradient[SPAN_TOKENS:])
        current_values.append(extended_value_gradient[SPAN_TOKENS:])
        lead_keys.append(extended_key_gradient[:SPAN_TOKENS])
        preceding_values.append(extended_value_gradient[:SPAN_TOKENS])
    incoming = passed_along(jnp.stack([lead_keys[0], preceding_values[0]]), "tok", -1)
    tail_key, tail_value = (incoming[0], incoming[1])
    grad_keys, grad_values = ([], [])
    for index in range(span_count):
        later_key = lead_keys[index + 1] if index + 1 < span_count else tail_key
        later_value = preceding_values[index + 1] if index + 1 < span_count else tail_value
        grad_keys.append((own_keys[index] + later_key).astype(jnp.bfloat16))
        grad_values.append((current_values[index] + later_value).astype(jnp.bfloat16))
    return (
        jnp.concatenate(outputs, axis=0),
        jnp.concatenate(grad_qs, axis=0),
        jnp.concatenate(grad_keys, axis=0),
        jnp.concatenate(grad_values, axis=0),
    )


def solution(mesh):
    in_specs = (
        P("tok", "mem"),
        P("tok", "mem"),
        P("tok", "mem"),
        P("mem", "tok", None, None),
        P("tok", "mem", None),
        P("mem"),
        P("tok", "mem"),
    )
    out_specs = (P("tok", "mem"), P("tok", "mem"), P("tok", "mem"), P("tok", "mem"))
    return jax.shard_map(
        per_device, mesh=mesh, in_specs=in_specs, out_specs=out_specs, check_vma=False
    )
```

profile of v0, /device:TPU:11, one launch (start us, length us, event | category | flops | bytes accessed | tf_op | source)
XLA Modules:
  0.0 676.7 jit_solution(14694192521077037401)
XLA Ops:
  1.9 9.2 %all_to_all.17 = s32[8,1,16]{2,1,0:T(1,128)S(1)} all-to-all(s32[8,1,16]{2,1,0:T(1,128)S(1)} %bitcast.388), channel_id=1, replica_groups=mesh['mem'=4,'tok'=8] {'tok'}, dimensions={0} | all-to-all | bytes 1024 | tf_op jit(solution)/shard_map/all_to_all | solution.py:132
  11.2 9.9 %gather_fusion = bf16[128,128,256]{2,1,0:T(8,128)(2,1)} fusion(bf16[128,128,256]{2,1,0:T(8,128)(2,1)} %bitcast.372, s32[1024]{0:T(1024)S(1)} %pad_clamp_fusion.1), kind=kCustom, calls=%fused_computation | custom fusion | bytes 16777728 | tf_op jit(solution)/shard_map/gather | solution.py:132
  21.2 6.5 all-to-all-start.1
  27.7 2.9 copy.88
  30.5 4.6 copy.89
  38.0 3.5 collective-permute-start
  41.7 2.7 fusion.149
  45.7 2.7 fusion.147
  51.2 2.3 copy.126
  53.6 176.9 %collective-permute-done = bf16[2,512,1024]{1,2,0:T(8,128)(2,1)} collective-permute-done((bf16[2,512,1024]{1,2,0:T(8,128)(2,1)}, bf16[2,512,1024]{1,2,0:T(8,128)(2,1)}, u32[]{:S(2)}, u32[]{:S(2)}) %collective-permute-start) | collective-permute-done | bytes 2097184 | tf_op jit(solution)/shard_map/ppermute | solution.py:14
  236.1 6.2 gather_fusion.1
  242.3 4.0 fusion.146
  248.2 2.3 broadcast.326.clone.2
  250.5 2.3 broadcast.326.clone.3
  255.1 173.6 %while.32 = (s32[]{:T(128)}, bf16[8,512,128]{2,1,0:T(8,128)(2,1)}, bf16[8,512,128]{2,1,0:T(8,128)(2,1)}, f32[8,1024,128]{2,1,0:T(8,128)}, f32[8,1024,128]{2,1,0:...) while((s32[]{:T(128)}, bf16[8,512,128]{2,1,0:T(8,128)(2,1)}, ...), condition=%wide.region_9.10_spmd, body=%wide.region_2.9_spmd.sunk | while | flops 1091239424 | bytes 29934260 | solution.py:85
  260.2 2.0 fusion.229
  262.6 2.2 fusion.237
  269.6 2.0 fusion.236
  274.3 2.6 fusion.233
  282.0 2.0 fusion.229
  284.4 2.2 fusion.237
  296.1 2.6 fusion.233
  303.8 2.0 fusion.229
  306.2 2.2 fusion.237
  317.7 2.6 fusion.233
  325.4 2.0 fusion.229
  327.8 2.2 fusion.237
  339.4 2.6 fusion.233
  347.1 2.0 fusion.229
  349.5 2.2 fusion.237
  356.5 2.0 fusion.236
  361.1 2.6 fusion.233
  368.8 2.0 fusion.229
  371.2 2.2 fusion.237
  382.8 2.6 fusion.233
  390.5 2.0 fusion.229
  392.9 2.2 fusion.237
  399.9 2.0 fusion.236
  404.5 2.6 fusion.233
  412.2 2.0 fusion.229
  414.6 2.2 fusion.237
  426.2 2.6 fusion.233
  428.8 3.1 fusion.150
  431.9 2.3 broadcast.326.clone
  434.2 2.3 broadcast.326.clone.1
  438.7 160.9 %while.33 = (s32[]{:T(128)}, bf16[8,512,128]{2,1,0:T(8,128)(2,1)}, bf16[8,512,128]{2,1,0:T(8,128)(2,1)}, f32[8,1024,128]{2,1,0:T(8,128)}, f32[8,1024,128]{2,1,0:...) while((s32[]{:T(128)}, bf16[8,512,128]{2,1,0:T(8,128)(2,1)}, ...), condition=%wide.region_17.18_spmd, body=%wide.region_10.17_spmd.sunk | while | flops 1091761664 | bytes 29930156 | solution.py:85
  456.2 2.6 fusion.257
  476.4 2.6 fusion.257
  496.5 2.6 fusion.257
  516.6 2.6 fusion.257
  536.7 2.5 fusion.257
  556.8 2.6 fusion.257
  576.9 2.6 fusion.257
  584.0 2.0 fusion.253
  597.0 2.6 fusion.257
  599.6 4.0 fusion.134
  603.5 2.5 copy.111
  606.1 2.7 stack.21
  608.8 5.7 fusion.135
  614.5 2.5 copy.112
  617.0 2.7 stack.22
  619.7 2.6 pad_maximum_fusion
  622.3 2.2 collective-permute-start.1
  630.8 42.1 %collective-permute-done.1 = f32[2,512,1024]{2,1,0:T(8,128)S(1)} collective-permute-done((f32[2,512,1024]{2,1,0:T(8,128)S(1)}, f32[2,512,1024]{2,1,0:T(8,128)S(1)}, u32[]{:S(2)}, u32[]{:S(2)}) %collective-permute-start.1) | collective-permute-done | bytes 4194336 | tf_op jit(solution)/shard_map/ppermute | solution.py:14
  (301 shorter events, 270.9 us)
Async XLA Ops:
  21.2 214.9 %all-to-all-start.1 = ((bf16[8,16,128,256]{3,2,1,0:T(8,128)(2,1)}), bf16[8,16,128,256]{3,2,1,0:T(8,128)(2,1)}, u32[]{:S(2)}, u32[]{:S(2)}) async-start(bf16[8,16,128,256]{3,2,1,0:T(8,128)(2,1)} %bitcast.365), calls=%async_computation.1 | async-start | bytes 16777216 | tf_op jit(solution)/shard_map/all_to_all | solution.py:133
  30.5 201.7 %copy-start = (bf16[1024,1024]{0,1:T(8,128)(2,1)}, bf16[1024,1024]{0,1:T(8,128)(2,1)S(1)}, u32[]{:S(2)}) copy-start(bf16[1024,1024]{0,1:T(8,128)(2,1)S(1)} %copy.88) | copy-start | bytes 6291460
  38.0 192.5 %collective-permute-start = (bf16[2,512,1024]{1,2,0:T(8,128)(2,1)}, bf16[2,512,1024]{1,2,0:T(8,128)(2,1)}, u32[]{:S(2)}, u32[]{:S(2)}) collective-permute-start(bf16[2,512,1024]{1,2,0:T(8,128)(2,1)} %pad_maximum_fusion.3), channel_id=1, source_target_pairs={{0,1},{1,2},{2,3},{3,4},{4,5},{5,6},{6,7},{8,9},{9,10},{10,11},{11... | collective-permute-start | bytes 6291464 | tf_op jit(solution)/shard_map/ppermute | solution.py:14
  49.7 3.9 copy-start.8
  232.2 2.4 copy-start.1
  619.7 4.8 copy-start.7
  622.3 50.6 %collective-permute-start.1 = (f32[2,512,1024]{2,1,0:T(8,128)S(1)}, f32[2,512,1024]{2,1,0:T(8,128)S(1)}, u32[]{:S(2)}, u32[]{:S(2)}) collective-permute-start(f32[2,512,1024]{2,1,0:T(8,128)S(1)} %pad_maximum_fusion), channel_id=1, source_target_pairs={{1,0},{2,1},{3,2},{4,3},{5,4},{6,5},{7,6},{9,8},{10,9},{11,10},{12... | collective-permute-start | bytes 12582920 | tf_op jit(solution)/shard_map/ppermute | solution.py:14
  624.5 1.2 copy-start.6
  624.8 1.3 copy-start.4
  626.3 1.5 copy-start.5
  627.8 1.2 copy-start.3
  629.2 43.7 %copy-start.2 = (f32[8,64,8,128]{3,2,1,0:T(8,128)S(1)}, f32[8,64,8,128]{3,2,1,0:T(8,128)}, u32[]{:S(2)}) copy-start(f32[8,64,8,128]{3,2,1,0:T(8,128)} %get-tuple-element.294) | copy-start | bytes 6291460
where the time goes:
time: 682 us; the launch traced here: 677 us
  matrix products  274 us (40%)
  waiting for transfers between devices  219 us (32%)
  local copies, waits for them, and re-layouts  103 us (15%)
  other arithmetic  46.4 us (7%)
  starting transfers between devices  12.2 us (2%)
  loops' own time  11.4 us (2%)
  blocking collectives  9.21 us (1%)
    ppermute x2, waiting for transfers between devices, passed_along(): return lax.ppermute(block, axis, route)  219 us
    dot_general x16, matrix products, head_pass(): mem_out = jnp.dot(mem_probs, mem_values, preferred_element_type=jnp.float32)  41.3 us
    dot_general x16, matrix products, head_pass(): jnp.dot(local_gradient, values_ext.T, preferred_element_type=jnp.float32)  31.8 us
    dot_general x16, matrix products, head_pass(): jnp.dot(mem_dscores, mem_keys, preferred_element_type=jnp.float32)  31.3 us
    dot_general x16, matrix products, head_pass(): jnp.dot(grad_mem, mem_values.T, preferred_element_type=jnp.float32)  30.5 us
    dot_general x16, matrix products, head_pass(): jnp.dot(local_dscores.T, query, preferred_element_type=jnp.float32)  27.8 us
    dot_general x16, matrix products, head_pass(): jnp.dot(query, keys_ext.T, preferred_element_type=jnp.float32) * scaling  27 us
    dynamic_slice x48, local copies, waits for them, and re-layouts, span_sweep(): lax.map(per_head, (split_heads(query, head_count), split_heads(keys_ext,...  26.7 us
  transfers between devices with their start and end apart: 3, of which 2 were waited for; matrix products, arithmetic and copies ran while one was open for 5% of the time, Pallas kernels for 0%

commit v1 on v0

v1 whole, which is shorter than its diff:
```python
import functools

import jax
import jax.numpy as jnp
from jax import lax
from jax.experimental import pallas as pl
from jax.experimental.pallas import tpu as pltpu
from jax.sharding import PartitionSpec as P

SPAN = 512
HALF = 256
BLOCK = 128
R = 4
HD = 128
NEG = -1e30
ANY = pl.BlockSpec(memory_space=pl.ANY)
SMEM = pl.BlockSpec(memory_space=pltpu.SMEM)


def passed_along(block, axis, distance):
    devices = range(lax.axis_size(axis))
    route = [(i - distance, i) for i in devices if i - distance in devices]
    return lax.ppermute(block, axis, route)


def mm(a, b, dims):
    return lax.dot_general(a, b, (dims, ((), ())), preferred_element_type=jnp.float32)


def local_kernel(head, n_any, gates, prev_ok, q_ref, k_ref, v_ref, g_ref, hk_ref, hv_ref, *rest):
    (lo_ref, dq_ref, dk_ref, dv_ref, dkx_ref, dvx_ref, hdk_ref, hdv_ref, token_ref,
     kx, vx, kt, vt, acc_k, acc_v) = rest[n_any:]
    scaling = HD ** -0.5
    keep = 1.0 - gates[head]
    kx[:SPAN] = hk_ref[...]
    kx[SPAN:] = k_ref[...]
    vx[:SPAN] = hv_ref[...]
    vx[SPAN:] = v_ref[...]
    kt[...] = kx[...].T
    vt[...] = vx[...].T
    ok = prev_ok[0] > 0
    tri = (lax.broadcasted_iota(jnp.int32, (HALF, HALF), 0)
           <= lax.broadcasted_iota(jnp.int32, (HALF, HALF), 1))
    for span in range(2):
        for half in range(2):
            row0 = span * SPAN + half * HALF
            win0 = span * SPAN
            width = SPAN + HALF * (half + 1)
            rows = pl.ds(row0, HALF)
            win = pl.ds(win0, width)
            q = q_ref[rows, :]
            gl = (keep * g_ref[rows, :].astype(jnp.float32)).astype(jnp.bfloat16)
            st = mm(kx[win, :], q, ((1,), (1,))) * scaling
            first = st[:SPAN]
            if span == 0:
                first = jnp.where(ok, first, NEG)
            parts = [first]
            if half:
                parts.append(st[SPAN:width - HALF])
            parts.append(jnp.where(tri, st[width - HALF:], NEG))
            st = jnp.concatenate(parts, axis=0)
            top = jnp.max(st, axis=0, keepdims=True)
            e = jnp.exp(st - top)
            total = jnp.sum(e, axis=0, keepdims=True)
            pt = (e * (1.0 / total)).astype(jnp.bfloat16)
            out_t = mm(vt[:, win], pt, ((1,), (0,)))
            gt = gl.astype(jnp.float32).T
            dot = jnp.sum(gt * out_t, axis=0, keepdims=True)
            dpt = mm(vx[win, :], gl, ((1,), (1,)))
            dst = (pt.astype(jnp.float32) * (dpt - dot)).astype(jnp.bfloat16)
            dq_t = mm(kt[:, win], dst, ((1,), (0,)))
            lo_ref[rows, :] = keep * out_t.T
            dq_ref[rows, :] = scaling * dq_t.T
            dkw = mm(dst, q, ((1,), (0,)))
            dvw = mm(pt, gl, ((1,), (0,)))
            if span == 0 and half == 0:
                acc_k[win, :] = dkw
                acc_v[win, :] = dvw
            else:
                old = 768 if span == 0 else (1024 if half == 0 else 1280)
                seen = max(0, min(old, win0 + width) - win0)
                acc_k[pl.ds(win0, seen), :] += dkw[:seen]
                acc_v[pl.ds(win0, seen), :] += dvw[:seen]
                if seen < width:
                    acc_k[pl.ds(win0 + seen, width - seen), :] = dkw[seen:]
                    acc_v[pl.ds(win0 + seen, width - seen), :] = dvw[seen:]
    hdk_ref[...] = (scaling * acc_k[:SPAN]).astype(jnp.bfloat16)
    hdv_ref[...] = acc_v[:SPAN].astype(jnp.bfloat16)
    dk_ref[...] = (scaling * acc_k[SPAN:2 * SPAN]).astype(jnp.bfloat16)
    dv_ref[...] = acc_v[SPAN:2 * SPAN].astype(jnp.bfloat16)
    dkx_ref[...] = scaling * acc_k[2 * SPAN:]
    dvx_ref[...] = acc_v[2 * SPAN:]
    token_ref[...] = jnp.zeros_like(token_ref)


def local_head(head, gates, prev_ok, q, k, v, g, hk, hv, carry, after):
    rows, width = q.shape
    col = pl.BlockSpec((rows, HD), lambda i: (0, head))
    col_half = pl.BlockSpec((SPAN, HD), lambda i: (0, head))
    alone = pl.BlockSpec((SPAN, HD), lambda i: (0, 0))
    shapes = [
        jax.ShapeDtypeStruct((rows, width), jnp.float32),
        jax.ShapeDtypeStruct((rows, width), jnp.float32),
        jax.ShapeDtypeStruct((rows, width), jnp.bfloat16),
        jax.ShapeDtypeStruct((rows, width), jnp.bfloat16),
        jax.ShapeDtypeStruct((SPAN, width), jnp.float32),
        jax.ShapeDtypeStruct((SPAN, width), jnp.float32),
        jax.ShapeDtypeStruct((SPAN, HD), jnp.bfloat16),
        jax.ShapeDtypeStruct((SPAN, HD), jnp.bfloat16),
        jax.ShapeDtypeStruct((8, 128), jnp.float32),
    ]
    extra = list(carry) + list(after)
    result = pl.pallas_call(
        functools.partial(local_kernel, head, len(extra)),
        grid=(1,),
        out_shape=shapes,
        in_specs=[SMEM, SMEM, col, col, col, col, col_half, col_half] + [ANY] * len(extra),
        out_specs=[col, col, col_half, col_half, col_half, col_half, alone, alone,
                   pl.BlockSpec((8, 128), lambda i: (0, 0))],
        scratch_shapes=[
            pltpu.VMEM((3 * SPAN, HD), jnp.bfloat16),
            pltpu.VMEM((3 * SPAN, HD), jnp.bfloat16),
            pltpu.VMEM((HD, 3 * SPAN), jnp.bfloat16),
            pltpu.VMEM((HD, 3 * SPAN), jnp.bfloat16),
            pltpu.VMEM((3 * SPAN, HD), jnp.float32),
            pltpu.VMEM((3 * SPAN, HD), jnp.float32),
        ],
        input_output_aliases={8 + i: i for i in range(len(carry))},
        compiler_params=pltpu.CompilerParams(vmem_limit_bytes=32 * 2**20),
        cost_estimate=pl.CostEstimate(flops=6 * 2 * 2 * 512 * 896 * 128, bytes_accessed=4 * 2**20,
                                      transcendentals=2 * 512 * 896),
        name="local_head",
    )(gates, prev_ok, q, k, v, g, hk, hv, *extra)
    return result[:6], result[6], result[7], result[8]


def memory_kernel(counts, loc, gates, q_ref, g_ref, lo_ref, dqf_ref, dkx_ref, dvx_ref, ink_ref,
                  inv_ref, near, sib, pool, dk_in, dv_in, out_ref, dq_ref, dk_ref, dv_ref, buf,
                  sems):
    n_near, n_sib = counts
    head = pl.program_id(0)
    heads = pl.num_programs(0)
    scaling = HD ** -0.5

    def fetch(h, slot):
        for j in range(2 * R):
            index = loc[j // R, h, j % R]
            place = buf.at[slot, j]
            sem = sems.at[slot, j]

            @pl.when(index < n_near)
            def _():
                pltpu.make_async_copy(near.at[index], place, sem).start()

            @pl.when((index >= n_near) & (index < n_near + n_sib))
            def _():
                pltpu.make_async_copy(sib.at[index - n_near], place, sem).start()

            @pl.when(index >= n_near + n_sib)
            def _():
                pltpu.make_async_copy(pool.at[index - n_near - n_sib], place, sem).start()

    slot = lax.rem(head, 2)

    @pl.when(head == 0)
    def _():
        fetch(0, 0)

    @pl.when(head + 1 < heads)
    def _():
        fetch(head + 1, 1 - slot)

    dk_ref[...] = (dkx_ref[...] + ink_ref[...].astype(jnp.float32)).astype(jnp.bfloat16)
    dv_ref[...] = (dvx_ref[...] + inv_ref[...].astype(jnp.float32)).astype(jnp.bfloat16)
    for j in range(2 * R):
        pltpu.make_async_copy(near.at[0], buf.at[slot, j], sems.at[slot, j]).wait()
    gate = gates[head]
    for span in range(2):
        blocks = buf[slot, pl.ds(span * R, R)]
        mk = blocks[:, :, :HD].reshape(R * BLOCK, HD)
        mv = blocks[:, :, HD:].reshape(R * BLOCK, HD)
        for half in range(2):
            rows = pl.ds(span * SPAN + half * HALF, HALF)
            q = q_ref[rows, :]
            gm = (gate * g_ref[rows, :].astype(jnp.float32)).astype(jnp.bfloat16)
            s = mm(q, mk, ((1,), (1,))) * scaling
            top = jnp.max(s, axis=1, keepdims=True)
            e = jnp.exp(s - top)
            total = jnp.sum(e, axis=1, keepdims=True)
            p = (e * (1.0 / total)).astype(jnp.bfloat16)
            mo = mm(p, mv, ((1,), (0,)))
            dp = mm(gm, mv, ((1,), (1,)))
            dot = jnp.sum(gm.astype(jnp.float32) * mo, axis=1, keepdims=True)
            ds = (p.astype(jnp.float32) * (dp - dot)).astype(jnp.bfloat16)
            dqm = mm(ds, mk, ((1,), (0,)))
            out_ref[rows, :] = (gate * mo + lo_ref[rows, :]).astype(jnp.bfloat16)
            dq_ref[rows, :] = (scaling * dqm + dqf_ref[rows, :]).astype(jnp.bfloat16)


def memory_heads(loc, gates, q, g, carry, ink, inv, near, sib, pool):
    lo, dqf, dk, dv, dkx, dvx = carry
    rows, width = q.shape
    heads = width // HD
    col = pl.BlockSpec((rows, HD), lambda h: (0, h))
    col_half = pl.BlockSpec((SPAN, HD), lambda h: (0, h))
    lower = pl.BlockSpec((SPAN, HD), lambda h: (1, h))
    full = jax.ShapeDtypeStruct((rows, width), jnp.bfloat16)
    return pl.pallas_call(
        functools.partial(memory_kernel, (near.shape[0], sib.shape[0])),
        grid=(heads,),
        out_shape=[full] * 4,
        in_specs=[SMEM, SMEM, col, col, col, col, col_half, col_half, col_half, col_half]
        + [ANY] * 5,
        out_specs=[col, col, lower, lower],
        scratch_shapes=[
            pltpu.VMEM((2, 2 * R, BLOCK, 2 * HD), jnp.bfloat16),
            pltpu.SemaphoreType.DMA((2, 2 * R)),
        ],
        input_output_aliases={13: 2, 14: 3},
        compiler_params=pltpu.CompilerParams(vmem_limit_bytes=32 * 2**20),
        cost_estimate=pl.CostEstimate(flops=heads * 4 * 2 * 2 * 512 * 512 * 128,
                                      bytes_accessed=24 * 2**20,
                                      transcendentals=heads * 2 * 512 * 512),
        name="memory_heads",
    )(loc, gates, q, g, lo, dqf, dkx, dvx, ink, inv, near, sib, pool, dk, dv)


def exchange_all(memory, block_ids):
    tok_count = lax.axis_size("tok")
    heads_here, blocks_here = memory.shape[:2]
    wanted = block_ids.reshape(-1)
    request_count = wanted.shape[0]
    owner_rank = wanted // blocks_here
    head_index = jnp.arange(request_count) // R % heads_here
    request_code = head_index * blocks_here + wanted % blocks_here
    order_ids = jnp.arange(request_count)
    same_owner = owner_rank[:, None] == owner_rank[None, :]
    slot_index = jnp.sum(same_owner & (order_ids[None, :] < order_ids[:, None]), axis=1)
    capacity = 2 * request_count // tok_count
    to_owner = (owner_rank[:, None] == jnp.arange(tok_count)[None, :]).astype(jnp.int32)
    to_slot = (slot_index[:, None] == jnp.arange(capacity)[None, :]).astype(jnp.int32)
    request_table = jnp.sum(
        request_code[:, None, None] * to_owner[:, :, None] * to_slot[:, None, :], axis=0
    )
    mem_flat = memory.reshape(-1, BLOCK, memory.shape[-1])
    found = mem_flat[lax.all_to_all(request_table, "tok", split_axis=0, concat_axis=0, tiled=True)]
    returned = lax.all_to_all(found, "tok", split_axis=0, concat_axis=0, tiled=True)
    loc = (owner_rank * capacity + slot_index).reshape(block_ids.shape)
    return returned.reshape(-1, BLOCK, memory.shape[-1]), loc.astype(jnp.int32)


def per_device(queries, keys, values, memory, block_ids, gate_bias, grad_out):
    my_rank = lax.axis_index("tok")
    heads = gate_bias.shape[0]
    gates = jax.nn.sigmoid(gate_bias)
    prev_ok = (my_rank > 0).astype(jnp.int32).reshape(1)
    hk = passed_along(keys[-SPAN:], "tok", 1)
    hv = passed_along(values[-SPAN:], "tok", 1)
    returned, loc = exchange_all(memory, block_ids)
    carry, token = (), ()
    halo_k, halo_v = [], []
    for head in range(heads):
        carry, dk, dv, token = local_head(
            head, gates, prev_ok, queries, keys, values, grad_out, hk, hv, carry, token
        )
        token = (token,)
        halo_k.append(dk)
        halo_v.append(dv)
    ink = passed_along(jnp.concatenate(halo_k, axis=1), "tok", -1)
    inv = passed_along(jnp.concatenate(halo_v, axis=1), "tok", -1)
    return tuple(
        memory_heads(loc, gates, queries, grad_out, carry, ink, inv, returned, returned, returned)
    )


def solution(mesh):
    in_specs = (
        P("tok", "mem"),
        P("tok", "mem"),
        P("tok", "mem"),
        P("mem", "tok", None, None),
        P("tok", "mem", None),
        P("mem"),
        P("tok", "mem"),
    )
    out_specs = (P("tok", "mem"), P("tok", "mem"), P("tok", "mem"), P("tok", "mem"))
    return jax.shard_map(
        per_device, mesh=mesh, in_specs=in_specs, out_specs=out_specs, check_vma=False
    )
```

time: 682 us -> 377 us (0.55)
  matrix products: 274 us -> 0 us
  Pallas kernels: 0 us -> 90.3 us
  local copies, waits for them, and re-layouts: 103 us -> 44.3 us
  other arithmetic: 46.4 us -> 0.44 us
  loops' own time: 11.4 us -> 0 us
  waiting for transfers between devices: 219 us -> 212 us
    dot_general x160 -> x0, matrix products: 274 us -> none  [the longest x16 41.3 us: head_pass(): mem_out = jnp.dot(mem_probs, mem_values, preferred_element_type=jnp.float32)]
    pallas_call x0 -> x9, Pallas kernels: none -> 90.3 us  [the longest x8 61.4 us: local_head(): pl.pallas_call(functools.partial(local_kernel, head, len(extra)), grid=(1...]
    dynamic_slice x48 -> x0, local copies, waits for them, and re-layouts: 26.7 us -> none  [span_sweep(): lax.map(per_head, (split_heads(query, head_count), split_heads(keys_ext,...]
    another operation x11 -> x0, local copies, waits for them, and re-layouts: 20.6 us -> none
    reduce_sum x34 -> x2, other arithmetic: 16.3 us -> 0.38 us  [the longest x1 0.21 us: exchange_all(): jnp.sum(request_code[:, None, None] * to_owner[:, :, None] * to_slot[:, N...]
    slice x7 -> x2, local copies, waits for them, and re-layouts: 19.5 us -> 4.68 us  [the longest x1 2.41 us: per_device(): hk = passed_along(keys[-SPAN:], 'tok', 1)]
    another operation x2 -> x0, loops' own time: 11.4 us -> none  [span_sweep(): lax.map(per_head, (split_heads(query, head_count), split_heads(keys_ext,...]
    unnamed x25 -> x40, local copies, waits for them, and re-layouts: 17.4 us -> 28.2 us
  transfers between devices with their start and end apart: 3 -> 5, of which waited for: 2 -> 4; matrix products, arithmetic and copies ran while one was open for 5% -> 4% of each run, Pallas kernels for 0% -> 16%
where the time goes in v1:
time: 377 us; the launch traced here: 373 us
  waiting for transfers between devices  212 us (56%)
  Pallas kernels  90.3 us (24%)
  local copies, waits for them, and re-layouts  44.3 us (12%)
  starting transfers between devices  16 us (4%)
  blocking collectives  9.21 us (2%)
    ppermute x4, waiting for transfers between devices, passed_along(): return lax.ppermute(block, axis, route)  212 us
    pallas_call x8, Pallas kernels, local_head(): pl.pallas_call(functools.partial(local_kernel, head, len(extra)), grid=(1...  61.4 us
    pallas_call x1, Pallas kernels, memory_heads(): pl.pallas_call(functools.partial(memory_kernel, (near.shape[0], sib.shape...  28.9 us
    unnamed x40, local copies, waits for them, and re-layouts  28.2 us
    gather x1, local copies, waits for them, and re-layouts, exchange_all(): mem_flat[lax.all_to_all(request_table, 'tok', split_axis=0, concat_axis=0...  9.78 us
    ppermute x4, starting transfers between devices, passed_along(): return lax.ppermute(block, axis, route)  9.37 us
    all_to_all x1, blocking collectives, exchange_all(): lax.all_to_all(request_table, 'tok', split_axis=0, concat_axis=0, tiled=T...  9.21 us
  transfers between devices with their start and end apart: 5, of which 4 were waited for; matrix products, arithmetic and copies ran while one was open for 4% of the time, Pallas kernels for 16%

profile of v1, /device:TPU:11, one launch (start us, length us, event | category | flops | bytes accessed | tf_op | source)
XLA Modules:
  0.0 373.4 jit_solution(2235900726577128616)
XLA Ops:
  0.6 0.8 copy.71
  1.4 0.1 reshape.213
  1.5 0.2 convert_reduce_fusion
  1.7 0.2 multiply_reduce_fusion
  1.9 9.2 %all_to_all.17 = s32[8,1,16]{2,1,0:T(1,128)S(1)} all-to-all(s32[8,1,16]{2,1,0:T(1,128)S(1)} %bitcast.13), channel_id=1, replica_groups=mesh['mem'=4,'tok'=8] {'tok'}, dimensions={0} | all-to-all | bytes 1024 | tf_op jit(solution)/shard_map/all_to_all | solution.py:246
  11.1 0.1 reshape.222
  11.2 9.8 %gather_fusion = bf16[128,128,256]{2,1,0:T(8,128)(2,1)} fusion(bf16[128,128,256]{2,1,0:T(8,128)(2,1)} %bitcast.11, s32[1024]{0:T(1024)S(1)} %pad_clamp_fusion), kind=kCustom, calls=%fused_computation | custom fusion | bytes 16777728 | tf_op jit(solution)/shard_map/gather | solution.py:246
  21.0 6.6 %all-to-all-start.1 = ((bf16[8,16,128,256]{3,2,1,0:T(8,128)(2,1)}), bf16[8,16,128,256]{3,2,1,0:T(8,128)(2,1)}, u32[]{:S(2)}, u32[]{:S(2)}) async-start(bf16[8,16,128,256]{3,2,1,0:T(8,128)(2,1)} %bitcast.10), calls=%async_computation.1 | async-start | bytes 16777216 | tf_op jit(solution)/shard_map/all_to_all | solution.py:247
  27.6 0.0 copy-start.12
  27.6 0.0 copy-start.3
  27.6 2.4 slice.6
  30.0 3.3 collective-permute-start
  33.4 2.3 slice.7
  35.7 2.2 collective-permute-start.1
  37.9 0.0 copy-done.12
  37.9 181.3 %collective-permute-done.hk_ref = bf16[512,1024]{1,0:T(8,128)(2,1)S(1)} collective-permute-done((bf16[512,1024]{1,0:T(8,128)(2,1)}, bf16[512,1024]{1,0:T(8,128)(2,1)S(1)}, u32[]{:S(2)}, u32[]{:S(2)}) %collective-permute-start) | collective-permute-done | bytes 1048608 | tf_op jit(solution)/shard_map/ppermute | solution.py:23
  219.2 11.2 %collective-permute-done.1.hv_ref = bf16[512,1024]{1,0:T(8,128)(2,1)} collective-permute-done((bf16[512,1024]{1,0:T(8,128)(2,1)}, bf16[512,1024]{1,0:T(8,128)(2,1)}, u32[]{:S(2)}, u32[]{:S(2)}) %collective-permute-start.1) | collective-permute-done | bytes 1048608 | tf_op jit(solution)/shard_map/ppermute | solution.py:23
  230.5 0.0 copy-done.3
  230.5 0.0 copy-start.4
  230.5 1.6 copy-done.4
  232.1 0.0 copy-start.6
  232.1 1.6 copy-done.6
  233.7 0.0 copy-start.7
  233.7 1.6 copy-done.7
  235.2 7.6 %local_head.8 = (f32[1024,1024]{1,0:T(8,128)S(1)}, f32[1024,1024]{1,0:T(8,128)}, bf16[1024,1024]{1,0:T(8,128)(2,1)}, bf16[1024,1024]{1,0:T(8,128)(2,1)}, f32[512...) custom-call(f32[8]{0:T(128)S(1)} %add_divide_fusion.gates, ...), custom_call_target="tpu_custom_call" | custom-call | flops 1409286144 | bytes 4194304 | tf_op jit(solution)/shard_map/local_head/pallas_call | solution.py:113
  242.8 0.8 constant_dynamic-update-slice_fusion.7
  243.6 7.5 %local_head.9 = (f32[1024,1024]{1,0:T(8,128)S(1)}, f32[1024,1024]{1,0:T(8,128)}, bf16[1024,1024]{1,0:T(8,128)(2,1)}, bf16[1024,1024]{1,0:T(8,128)(2,1)}, f32[512...) custom-call(f32[8]{0:T(128)S(1)} %add_divide_fusion.gates, ...), custom_call_target="tpu_custom_call", output_to_operand_aliasing={{0}: (8, {}), {1}: (9, {}), {2}: (10, {}), {3}: (11, {}), {... | custom-call | flops 1409286144 | bytes 4194304 | tf_op jit(solution)/shard_map/local_head/pallas_call | solution.py:113
  251.1 0.7 constant_dynamic-update-slice_fusion.6
  251.8 7.8 %local_head.10 = (f32[1024,1024]{1,0:T(8,128)S(1)}, f32[1024,1024]{1,0:T(8,128)}, bf16[1024,1024]{1,0:T(8,128)(2,1)}, bf16[1024,1024]{1,0:T(8,128)(2,1)}, f32[51...) custom-call(f32[8]{0:T(128)S(1)} %add_divide_fusion.gates, ...), custom_call_target="tpu_custom_call", output_to_operand_aliasing={{0}: (8, {}), {1}: (9, {}), {2}: (10, {}), {3}: (11, {}), {... | custom-call | flops 1409286144 | bytes 4194304 | tf_op jit(solution)/shard_map/local_head/pallas_call | solution.py:113
  259.6 0.7 constant_dynamic-update-slice_fusion.5
  260.3 7.6 %local_head.11 = (f32[1024,1024]{1,0:T(8,128)S(1)}, f32[1024,1024]{1,0:T(8,128)}, bf16[1024,1024]{1,0:T(8,128)(2,1)}, bf16[1024,1024]{1,0:T(8,128)(2,1)}, f32[51...) custom-call(f32[8]{0:T(128)S(1)} %add_divide_fusion.gates, ...), custom_call_target="tpu_custom_call", output_to_operand_aliasing={{0}: (8, {}), {1}: (9, {}), {2}: (10, {}), {3}: (11, {}), {... | custom-call | flops 1409286144 | bytes 4194304 | tf_op jit(solution)/shard_map/local_head/pallas_call | solution.py:113
  267.9 0.7 constant_dynamic-update-slice_fusion.4
  268.6 8.0 %local_head.12 = (f32[1024,1024]{1,0:T(8,128)S(1)}, f32[1024,1024]{1,0:T(8,128)}, bf16[1024,1024]{1,0:T(8,128)(2,1)}, bf16[1024,1024]{1,0:T(8,128)(2,1)}, f32[51...) custom-call(f32[8]{0:T(128)S(1)} %add_divide_fusion.gates, ...), custom_call_target="tpu_custom_call", output_to_operand_aliasing={{0}: (8, {}), {1}: (9, {}), {2}: (10, {}), {3}: (11, {}), {... | custom-call | flops 1409286144 | bytes 4194304 | tf_op jit(solution)/shard_map/local_head/pallas_call | solution.py:113
  276.6 0.7 constant_dynamic-update-slice_fusion.3
  277.2 7.6 %local_head.13 = (f32[1024,1024]{1,0:T(8,128)S(1)}, f32[1024,1024]{1,0:T(8,128)}, bf16[1024,1024]{1,0:T(8,128)(2,1)}, bf16[1024,1024]{1,0:T(8,128)(2,1)}, f32[51...) custom-call(f32[8]{0:T(128)S(1)} %add_divide_fusion.gates, ...), custom_call_target="tpu_custom_call", output_to_operand_aliasing={{0}: (8, {}), {1}: (9, {}), {2}: (10, {}), {3}: (11, {}), {... | custom-call | flops 1409286144 | bytes 4194304 | tf_op jit(solution)/shard_map/local_head/pallas_call | solution.py:113
  284.8 0.7 constant_dynamic-update-slice_fusion.2
  285.5 7.6 %local_head.14 = (f32[1024,1024]{1,0:T(8,128)S(1)}, f32[1024,1024]{1,0:T(8,128)}, bf16[1024,1024]{1,0:T(8,128)(2,1)}, bf16[1024,1024]{1,0:T(8,128)(2,1)}, f32[51...) custom-call(f32[8]{0:T(128)S(1)} %add_divide_fusion.gates, ...), custom_call_target="tpu_custom_call", output_to_operand_aliasing={{0}: (8, {}), {1}: (9, {}), {2}: (10, {}), {3}: (11, {}), {... | custom-call | flops 1409286144 | bytes 4194304 | tf_op jit(solution)/shard_map/local_head/pallas_call | solution.py:113
  293.1 0.7 constant_dynamic-update-slice_fusion.1
  293.7 7.8 %local_head.15 = (f32[1024,1024]{1,0:T(8,128)S(1)}, f32[1024,1024]{1,0:T(8,128)}, bf16[1024,1024]{1,0:T(8,128)(2,1)}, bf16[1024,1024]{1,0:T(8,128)(2,1)}, f32[51...) custom-call(f32[8]{0:T(128)S(1)} %add_divide_fusion.gates, ...), custom_call_target="tpu_custom_call", output_to_operand_aliasing={{0}: (8, {}), {1}: (9, {}), {2}: (10, {}), {3}: (11, {}), {... | custom-call | flops 1409286144 | bytes 4194304 | tf_op jit(solution)/shard_map/local_head/pallas_call | solution.py:113
  301.5 0.0 copy-start
  301.5 1.9 copy-done
  303.4 0.0 copy-start.8
  303.4 1.3 copy-done.8
  304.8 1.3 copy-done.10
  306.1 0.7 constant_dynamic-update-slice_fusion
  306.8 1.9 collective-permute-start.2
  308.7 0.7 constant_dynamic-update-slice_fusion.14
  309.4 0.7 constant_dynamic-update-slice_fusion.13
  310.0 0.7 constant_dynamic-update-slice_fusion.12
  310.7 0.7 constant_dynamic-update-slice_fusion.11
  311.4 0.7 constant_dynamic-update-slice_fusion.10
  312.1 0.7 constant_dynamic-update-slice_fusion.9
  312.8 0.7 constant_dynamic-update-slice_fusion.8
  313.5 1.9 collective-permute-start.3
  315.4 0.1 reduce_sum.21
  315.5 8.3 %collective-permute-done.2.ink_ref = bf16[512,1024]{1,0:T(8,128)(2,1)S(1)} collective-permute-done((bf16[512,1024]{1,0:T(8,128)(2,1)}, bf16[512,1024]{1,0:T(8,128)(2,1)S(1)}, u32[]{:S(2)}, u32[]{:S(2)}) %collective-permute-start.2) | collective-permute-done | bytes 1048608 | tf_op jit(solution)/shard_map/ppermute | solution.py:23
  323.8 11.3 %collective-permute-done.3.inv_ref = bf16[512,1024]{1,0:T(8,128)(2,1)} collective-permute-done((bf16[512,1024]{1,0:T(8,128)(2,1)}, bf16[512,1024]{1,0:T(8,128)(2,1)}, u32[]{:S(2)}, u32[]{:S(2)}) %collective-permute-start.3) | collective-permute-done | bytes 1048608 | tf_op jit(solution)/shard_map/ppermute | solution.py:23
  335.2 0.0 all-to-all-done.1
  335.2 2.2 copy-done.1
  337.4 2.2 copy-done.2
  339.5 1.6 copy-done.5
  341.1 1.6 copy-done.9
  342.7 1.6 copy-done.11
  344.3 28.9 %memory_heads.1 = (bf16[1024,1024]{1,0:T(8,128)(2,1)}, bf16[1024,1024]{1,0:T(8,128)(2,1)}, bf16[1024,1024]{1,0:T(8,128)(2,1)}, bf16[1024,1024]{1,0:T(8,128)(2,1)}) custom-call(s32[2,8,4]{2,1,0:T(8,128)S(1)} %fusion.3.loc, f32[8]{0:T(128)S(1)} %add_divide_fusion.gates, ...), custom_call_target="tpu_custom_call", output_to_operand_aliasing={{2}: (13, {}), {3}: (14, {})} | custom-call | flops 4294967296 | bytes 25165824 | tf_op jit(solution)/shard_map/memory_heads/pallas_call | solution.py:208
  (13 shorter events, 0.1 us)
Async XLA Ops:
  21.0 314.1 %all-to-all-start.1 = ((bf16[8,16,128,256]{3,2,1,0:T(8,128)(2,1)}), bf16[8,16,128,256]{3,2,1,0:T(8,128)(2,1)}, u32[]{:S(2)}, u32[]{:S(2)}) async-start(bf16[8,16,128,256]{3,2,1,0:T(8,128)(2,1)} %bitcast.10), calls=%async_computation.1 | async-start | bytes 16777216 | tf_op jit(solution)/shard_map/all_to_all | solution.py:247
  27.6 10.3 %copy-start.12 = (f32[8]{0:T(128)S(1)}, f32[8]{0:T(128)}, u32[]{:S(2)}) copy-start(f32[8]{0:T(128)} %param.12) | copy-start | bytes 100
  27.6 202.8 %copy-start.3 = (bf16[1024,1024]{1,0:T(8,128)(2,1)S(1)}, bf16[1024,1024]{1,0:T(8,128)(2,1)}, u32[]{:S(2)}) copy-start(bf16[1024,1024]{1,0:T(8,128)(2,1)} %q_ref.17) | copy-start | bytes 6291460
  30.0 189.2 %collective-permute-start = (bf16[512,1024]{1,0:T(8,128)(2,1)}, bf16[512,1024]{1,0:T(8,128)(2,1)S(1)}, u32[]{:S(2)}, u32[]{:S(2)}) collective-permute-start(bf16[512,1024]{1,0:T(8,128)(2,1)} %slice.6), channel_id=1, source_target_pairs={{0,1},{1,2},{2,3},{3,4},{4,5},{5,6},{6,7},{8,9},{9,10},{10,11},{11... | collective-permute-start | bytes 3145736 | tf_op jit(solution)/shard_map/ppermute | solution.py:23
  35.7 194.8 %collective-permute-start.1 = (bf16[512,1024]{1,0:T(8,128)(2,1)}, bf16[512,1024]{1,0:T(8,128)(2,1)}, u32[]{:S(2)}, u32[]{:S(2)}) collective-permute-start(bf16[512,1024]{1,0:T(8,128)(2,1)} %slice.7), channel_id=1, source_target_pairs={{0,1},{1,2},{2,3},{3,4},{4,5},{5,6},{6,7},{8,9},{9,10},{10,11},{11... | collective-permute-start | bytes 3145736 | tf_op jit(solution)/shard_map/ppermute | solution.py:23
  230.5 1.6 copy-start.4
  232.1 1.6 copy-start.6
  233.7 1.6 copy-start.7
  301.5 1.9 copy-start
  303.4 1.3 copy-start.8
  304.8 1.3 copy-start.10
  306.8 17.1 %collective-permute-start.2 = (bf16[512,1024]{1,0:T(8,128)(2,1)}, bf16[512,1024]{1,0:T(8,128)(2,1)S(1)}, u32[]{:S(2)}, u32[]{:S(2)}) collective-permute-start(bf16[512,1024]{1,0:T(8,128)(2,1)} %constant_dynamic-update-slice_fusion), channel_id=1, source_target_pairs={{1,0},{2,1},{3,2},{4,3},{5,4},{6,5},{7,6},{9,8},{10,9},{11,10},{12... | collective-permute-start | bytes 3145736 | tf_op jit(solution)/shard_map/ppermute | solution.py:23
  313.5 21.7 %collective-permute-start.3 = (bf16[512,1024]{1,0:T(8,128)(2,1)}, bf16[512,1024]{1,0:T(8,128)(2,1)}, u32[]{:S(2)}, u32[]{:S(2)}) collective-permute-start(bf16[512,1024]{1,0:T(8,128)(2,1)} %constant_dynamic-update-slice_fusion.8), channel_id=1, source_target_pairs={{1,0},{2,1},{3,2},{4,3},{5,4},{6,5},{7,6},{9,8},{10,9},{11,10},{12... | collective-permute-start | bytes 3145736 | tf_op jit(solution)/shard_map/ppermute | solution.py:23
  335.2 2.2 copy-start.1
  337.3 2.2 copy-start.2
  339.5 1.6 copy-start.5
  341.1 1.6 copy-start.9
  342.7 1.6 copy-start.11

commit v2 on v1

--- a/solution.py
+++ b/solution.py
@@ -13,6 +13,10 @@
 R = 4
 HD = 128
 NEG = -1e30
+KIND = 512
+VMEM_LIMIT = 56 * 2**20
+BASE = 22
+EXTRA = 10
 ANY = pl.BlockSpec(memory_space=pl.ANY)
 SMEM = pl.BlockSpec(memory_space=pltpu.SMEM)
 
@@ -27,14 +31,14 @@
     return lax.dot_general(a, b, (dims, ((), ())), preferred_element_type=jnp.float32)
 
 
-def local_kernel(head, n_any, gates, prev_ok, q_ref, k_ref, v_ref, g_ref, hk_ref, hv_ref, *rest):
-    (lo_ref, dq_ref, dk_ref, dv_ref, dkx_ref, dvx_ref, hdk_ref, hdv_ref, token_ref,
+def local_kernel(head, n_any, gates, prev_ok, q_ref, k_ref, v_ref, g_ref, halo_ref, *rest):
+    (lo_ref, dq_ref, dk_ref, dv_ref, dkx_ref, dvx_ref, back_ref, token_ref,
      kx, vx, kt, vt, acc_k, acc_v) = rest[n_any:]
     scaling = HD ** -0.5
     keep = 1.0 - gates[head]
-    kx[:SPAN] = hk_ref[...]
+    kx[:SPAN] = halo_ref[:SPAN]
     kx[SPAN:] = k_ref[...]
-    vx[:SPAN] = hv_ref[...]
+    vx[:SPAN] = halo_ref[SPAN:]
     vx[SPAN:] = v_ref[...]
     kt[...] = kx[...].T
     vt[...] = vx[...].T
@@ -84,8 +88,8 @@
                 if seen < width:
                     acc_k[pl.ds(win0 + seen, width - seen), :] = dkw[seen:]
                     acc_v[pl.ds(win0 + seen, width - seen), :] = dvw[seen:]
-    hdk_ref[...] = (scaling * acc_k[:SPAN]).astype(jnp.bfloat16)
-    hdv_ref[...] = acc_v[:SPAN].astype(jnp.bfloat16)
+    back_ref[:SPAN] = (scaling * acc_k[:SPAN]).astype(jnp.bfloat16)
+    back_ref[SPAN:] = acc_v[:SPAN].astype(jnp.bfloat16)
     dk_ref[...] = (scaling * acc_k[SPAN:2 * SPAN]).astype(jnp.bfloat16)
     dv_ref[...] = acc_v[SPAN:2 * SPAN].astype(jnp.bfloat16)
     dkx_ref[...] = scaling * acc_k[2 * SPAN:]
@@ -93,11 +97,10 @@
     token_ref[...] = jnp.zeros_like(token_ref)
 
 
-def local_head(head, gates, prev_ok, q, k, v, g, hk, hv, carry, after):
+def local_head(head, gates, prev_ok, q, k, v, g, halo, carry, after):
     rows, width = q.shape
     col = pl.BlockSpec((rows, HD), lambda i: (0, head))
     col_half = pl.BlockSpec((SPAN, HD), lambda i: (0, head))
-    alone = pl.BlockSpec((SPAN, HD), lambda i: (0, 0))
     shapes = [
         jax.ShapeDtypeStruct((rows, width), jnp.float32),
         jax.ShapeDtypeStruct((rows, width), jnp.float32),
@@ -105,8 +108,7 @@
         jax.ShapeDtypeStruct((rows, width), jnp.bfloat16),
         jax.ShapeDtypeStruct((SPAN, width), jnp.float32),
         jax.ShapeDtypeStruct((SPAN, width), jnp.float32),
-        jax.ShapeDtypeStruct((SPAN, HD), jnp.bfloat16),
-        jax.ShapeDtypeStruct((SPAN, HD), jnp.bfloat16),
+        jax.ShapeDtypeStruct((2 * SPAN, width), jnp.bfloat16),
         jax.ShapeDtypeStruct((8, 128), jnp.float32),
     ]
     extra = list(carry) + list(after)
@@ -114,8 +116,8 @@
         functools.partial(local_kernel, head, len(extra)),
         grid=(1,),
         out_shape=shapes,
-        in_specs=[SMEM, SMEM, col, col, col, col, col_half, col_half] + [ANY] * len(extra),
-        out_specs=[col, col, col_half, col_half, col_half, col_half, alone, alone,
+        in_specs=[SMEM, SMEM, col, col, col, col, col] + [ANY] * len(extra),
+        out_specs=[col, col, col_half, col_half, col_half, col_half, col,
                    pl.BlockSpec((8, 128), lambda i: (0, 0))],
         scratch_shapes=[
             pltpu.VMEM((3 * SPAN, HD), jnp.bfloat16),
@@ -125,40 +127,45 @@
             pltpu.VMEM((3 * SPAN, HD), jnp.float32),
             pltpu.VMEM((3 * SPAN, HD), jnp.float32),
         ],
-        input_output_aliases={8 + i: i for i in range(len(carry))},
-        compiler_params=pltpu.CompilerParams(vmem_limit_bytes=32 * 2**20),
-        cost_estimate=pl.CostEstimate(flops=6 * 2 * 2 * 512 * 896 * 128, bytes_accessed=4 * 2**20,
+        input_output_aliases={7 + i: i for i in range(len(carry))},
+        compiler_params=pltpu.CompilerParams(vmem_limit_bytes=VMEM_LIMIT),
+        cost_estimate=pl.CostEstimate(flops=9 * 10**9, bytes_accessed=4 * 2**20,
                                       transcendentals=2 * 512 * 896),
         name="local_head",
-    )(gates, prev_ok, q, k, v, g, hk, hv, *extra)
-    return result[:6], result[6], result[7], result[8]
-
-
-def memory_kernel(counts, loc, gates, q_ref, g_ref, lo_ref, dqf_ref, dkx_ref, dvx_ref, ink_ref,
-                  inv_ref, near, sib, pool, dk_in, dv_in, out_ref, dq_ref, dk_ref, dv_ref, buf,
-                  sems):
-    n_near, n_sib = counts
+    )(gates, prev_ok, q, k, v, g, halo, *extra)
+    return result[:7], result[7]
+
+
+def memory_kernel(n_src, loc, gates, q_ref, g_ref, lo_ref, dqf_ref, dkx_ref, dvx_ref, back_ref,
+                  dk_in, dv_in, *rest):
+    sources = rest[:n_src]
+    out_ref, dq_ref, dk_ref, dv_ref, buf, sems = rest[n_src:]
     head = pl.program_id(0)
     heads = pl.num_programs(0)
     scaling = HD ** -0.5
 
     def fetch(h, slot):
         for j in range(2 * R):
-            index = loc[j // R, h, j % R]
-            place = buf.at[slot, j]
-            sem = sems.at[slot, j]
-
-            @pl.when(index < n_near)
-            def _():
-                pltpu.make_async_copy(near.at[index], place, sem).start()
-
-            @pl.when((index >= n_near) & (index < n_near + n_sib))
-            def _():
-                pltpu.make_async_copy(sib.at[index - n_near], place, sem).start()
-
-            @pl.when(index >= n_near + n_sib)
-            def _():
-                pltpu.make_async_copy(pool.at[index - n_near - n_sib], place, sem).start()
+            code = loc[j // R, h, j % R]
+            kind, index = code // KIND, lax.rem(code, KIND)
+
+            def pick(low, high):
+                if high - low == 1:
+                    pltpu.make_async_copy(
+                        sources[low].at[index], buf.at[slot, j], sems.at[slot, j]
+                    ).start()
+                    return
+                middle = (low + high) // 2
+
+                @pl.when(kind < middle)
+                def _():
+                    pick(low, middle)
+
+                @pl.when(kind >= middle)
+                def _():
+                    pick(middle, high)
+
+            pick(0, n_src)
 
     slot = lax.rem(head, 2)
 
@@ -170,10 +177,10 @@
     def _():
         fetch(head + 1, 1 - slot)
 
-    dk_ref[...] = (dkx_ref[...] + ink_ref[...].astype(jnp.float32)).astype(jnp.bfloat16)
-    dv_ref[...] = (dvx_ref[...] + inv_ref[...].astype(jnp.float32)).astype(jnp.bfloat16)
+    dk_ref[...] = (dkx_ref[...] + back_ref[:SPAN].astype(jnp.float32)).astype(jnp.bfloat16)
+    dv_ref[...] = (dvx_ref[...] + back_ref[SPAN:].astype(jnp.float32)).astype(jnp.bfloat16)
     for j in range(2 * R):
-        pltpu.make_async_copy(near.at[0], buf.at[slot, j], sems.at[slot, j]).wait()
+        pltpu.make_async_copy(sources[0].at[0], buf.at[slot, j], sems.at[slot, j]).wait()
     gate = gates[head]
     for span in range(2):
         blocks = buf[slot, pl.ds(span * R, R)]
@@ -197,8 +204,8 @@
             dq_ref[rows, :] = (scaling * dqm + dqf_ref[rows, :]).astype(jnp.bfloat16)
 
 
-def memory_heads(loc, gates, q, g, carry, ink, inv, near, sib, pool):
-    lo, dqf, dk, dv, dkx, dvx = carry
+def memory_heads(loc, gates, q, g, carry, back, sources):
+    lo, dqf, dk, dv, dkx, dvx = carry[:6]
     rows, width = q.shape
     heads = width // HD
     col = pl.BlockSpec((rows, HD), lambda h: (0, h))
@@ -206,23 +213,23 @@
     lower = pl.BlockSpec((SPAN, HD), lambda h: (1, h))
     full = jax.ShapeDtypeStruct((rows, width), jnp.bfloat16)
     return pl.pallas_call(
-        functools.partial(memory_kernel, (near.shape[0], sib.shape[0])),
+        functools.partial(memory_kernel, len(sources)),
         grid=(heads,),
         out_shape=[full] * 4,
-        in_specs=[SMEM, SMEM, col, col, col, col, col_half, col_half, col_half, col_half]
-        + [ANY] * 5,
+        in_specs=[SMEM, SMEM, col, col, col, col, col_half, col_half, col]
+        + [ANY] * (2 + len(sources)),
         out_specs=[col, col, lower, lower],
         scratch_shapes=[
             pltpu.VMEM((2, 2 * R, BLOCK, 2 * HD), jnp.bfloat16),
             pltpu.SemaphoreType.DMA((2, 2 * R)),
         ],
-        input_output_aliases={13: 2, 14: 3},
-        compiler_params=pltpu.CompilerParams(vmem_limit_bytes=32 * 2**20),
+        input_output_aliases={9: 2, 10: 3},
+        compiler_params=pltpu.CompilerParams(vmem_limit_bytes=VMEM_LIMIT),
         cost_estimate=pl.CostEstimate(flops=heads * 4 * 2 * 2 * 512 * 512 * 128,
                                       bytes_accessed=24 * 2**20,
                                       transcendentals=heads * 2 * 512 * 512),
         name="memory_heads",
-    )(loc, gates, q, g, lo, dqf, dkx, dvx, ink, inv, near, sib, pool, dk, dv)
+    )(loc, gates, q, g, lo, dqf, dkx, dvx, back, dk, dv, *sources)
 
 
 def exchange_all(memory, block_ids):
@@ -249,27 +256,217 @@
     return returned.reshape(-1, BLOCK, memory.shape[-1]), loc.astype(jnp.int32)
 
 
+def pack_kernel(lists, n_any, table, near, *rest):
+    outs = rest[n_any:n_any + len(lists)]
+    held, sems, sent = rest[-3:]
+    for phase in range(2):
+        number = 0
+        for place, (row, start, count) in enumerate(lists):
+            for j in range(count):
+                code = table[row, start + j]
+
+                @pl.when(code >= 0)
+                def _():
+                    copy = pltpu.make_async_copy(near.at[code], held.at[number], sems.at[number])
+                    copy.wait() if phase else copy.start()
+                number += 1
+            if phase:
+                pltpu.make_async_copy(
+                    held.at[pl.ds(number - count, count)], outs[place], sent.at[place]
+                ).start()
+    number = 0
+    for place, (row, start, count) in enumerate(lists):
+        pltpu.make_async_copy(
+            held.at[pl.ds(number, count)], outs[place], sent.at[place]
+        ).wait()
+        number += count
+
+
+def pack(table, near, lists, after):
+    total = sum(count for row, start, count in lists)
+    return pl.pallas_call(
+        functools.partial(pack_kernel, lists, len(after)),
+        out_shape=[jax.ShapeDtypeStruct((n,) + near.shape[1:], near.dtype) for _, _, n in lists],
+        in_specs=[SMEM, ANY] + [ANY] * len(after),
+        out_specs=[ANY] * len(lists),
+        scratch_shapes=[
+            pltpu.VMEM((total,) + near.shape[1:], near.dtype),
+            pltpu.SemaphoreType.DMA((total,)),
+            pltpu.SemaphoreType.DMA((len(lists),)),
+        ],
+        compiler_params=pltpu.CompilerParams(vmem_limit_bytes=VMEM_LIMIT),
+        cost_estimate=pl.CostEstimate(flops=0, bytes_accessed=total * 2**17, transcendentals=0),
+        name="pack",
+    )(table, near, *after)
+
+
+def tails(keys, values, after):
+    width = keys.shape[1]
+    block = pl.BlockSpec((SPAN, width), lambda i: (keys.shape[0] // SPAN - 1, 0))
+
+    def kernel(k_ref, v_ref, after_ref, out_ref):
+        out_ref[:SPAN] = k_ref[...]
+        out_ref[SPAN:] = v_ref[...]
+
+    return pl.pallas_call(
+        kernel,
+        grid=(1,),
+        out_shape=jax.ShapeDtypeStruct((2 * SPAN, width), keys.dtype),
+        in_specs=[block, block, ANY],
+        out_specs=pl.BlockSpec((2 * SPAN, width), lambda i: (0, 0)),
+        compiler_params=pltpu.CompilerParams(vmem_limit_bytes=VMEM_LIMIT),
+        name="tails",
+    )(keys, values, after)
+
+
+def summed(parts, after):
+    def kernel(*refs):
+        total = refs[0][...]
+        for ref in refs[1:len(parts)]:
+            total = total + ref[...]
+        refs[-1][...] = total
+
+    x = parts[0]
+    whole = pl.BlockSpec(memory_space=pltpu.VMEM)
+    return pl.pallas_call(
+        kernel,
+        out_shape=jax.ShapeDtypeStruct(x.shape, x.dtype),
+        in_specs=[whole] * len(parts) + [ANY] * len(after),
+        out_specs=whole,
+        compiler_params=pltpu.CompilerParams(vmem_limit_bytes=VMEM_LIMIT),
+        name="summed",
+    )(*parts, *after)
+
+
+def plan(block_ids, everyone, heads, blocks_here):
+    tok_count = lax.axis_size("tok")
+    chips = tok_count // 2
+    shard = heads * blocks_here
+    here = lax.axis_index("tok")
+    chip, core = here // 2, here % 2
+    head_of = jnp.arange(heads, dtype=jnp.int32)[None, :, None]
+    block = (everyone // blocks_here) * shard + head_of * blocks_here + everyone % blocks_here
+    universe = jnp.arange(tok_count * shard, dtype=jnp.int32)
+    each = jnp.any(block.reshape(tok_count, -1)[:, :, None] == universe, axis=1)
+    need = each.reshape(chips, 2, -1).any(axis=1).reshape(chips, tok_count, shard)
+    sibling = lax.dynamic_slice(each, (here ^ 1, here * shard), (1, shard))
+    away = jnp.arange(chips)[:, None] != jnp.arange(tok_count)[None, :] // 2
+    most = jnp.max(jnp.sum(need.astype(jnp.int32), axis=2) * away, axis=0)
+    before = jnp.triu(jnp.ones((shard, shard), jnp.bfloat16), 1)
+
+    def ranked(wanted):
+        rank = jnp.dot(wanted.astype(jnp.bfloat16), before, preferred_element_type=jnp.float32)
+        return jnp.where(wanted, rank.astype(jnp.int32), -1)
+
+    rank = ranked(need)
+    from_me = lax.dynamic_index_in_dim(rank, here, 1, keepdims=False)
+    sent = jnp.concatenate(
+        [ranked(sibling)]
+        + [lax.dynamic_slice_in_dim(from_me, (chip + k) % chips, 1, 0) for k in range(1, chips)]
+    )
+    slot = jnp.arange(BASE + EXTRA, dtype=jnp.int32)
+    hit = sent[:, None, :] == slot[None, :, None]
+    table = jnp.sum(jnp.where(hit, jnp.arange(1, shard + 1, dtype=jnp.int32), 0), axis=2) - 1
+    sender = jnp.arange(tok_count, dtype=jnp.int32)[:, None]
+    got = lax.dynamic_index_in_dim(rank, chip, 0, keepdims=False)
+    away_by = (chip - sender // 2) % chips
+    kind = jnp.where(got < BASE, 2 * away_by + (sender + core) % 2, 2 * chips)
+    place = kind * KIND + jnp.where(got < BASE, got, got - BASE)
+    mine = ranked(lax.dynamic_slice(each, (here, (here ^ 1) * shard), (1, shard)))
+    place = jnp.where(sender == here, jnp.arange(shard, dtype=jnp.int32), place)
+    place = jnp.where(sender == here ^ 1, KIND + mine, place).reshape(-1)
+    own = (block_ids // blocks_here) * shard + head_of * blocks_here + block_ids % blocks_here
+    loc = jnp.sum(jnp.where(own.reshape(-1, 1) == universe, place, 0), axis=1)
+    return table, loc.reshape(block_ids.shape), most
+
+
+def chip_shift(block, distance, only=None):
+    count = lax.axis_size("tok")
+    route = [(i, (i + 2 * distance) % count) for i in range(count) if only in (None, i)]
+    return lax.ppermute(block, "tok", route)
+
+
+def core_swap(block):
+    return lax.ppermute(block, "tok", [(i, i ^ 1) for i in range(lax.axis_size("tok"))])
+
+
+def most_of_all(most):
+    count = lax.axis_size("mem")
+    step = 1
+    while step < count:
+        other = lax.ppermute(most, "mem", [(i, i ^ step) for i in range(count)])
+        most = jnp.maximum(most, other)
+        step *= 2
+    return most[:, 0]
+
+
 def per_device(queries, keys, values, memory, block_ids, gate_bias, grad_out):
     my_rank = lax.axis_index("tok")
-    heads = gate_bias.shape[0]
+    tok_count = lax.axis_size("tok")
+    heads, blocks_here = memory.shape[:2]
+    chips = tok_count // 2
+    direct = chips == 4 and lax.axis_size("mem") == 4
     gates = jax.nn.sigmoid(gate_bias)
     prev_ok = (my_rank > 0).astype(jnp.int32).reshape(1)
-    hk = passed_along(keys[-SPAN:], "tok", 1)
-    hv = passed_along(values[-SPAN:], "tok", 1)
-    returned, loc = exchange_all(memory, block_ids)
+    if direct:
+        everyone = lax.all_to_all(
+            jnp.broadcast_to(block_ids[None], (tok_count,) + block_ids.shape),
+            "tok", split_axis=0, concat_axis=0, tiled=True,
+        )
+    tail = tails(keys, values, everyone if direct else block_ids)
+    halo = passed_along(tail, "tok", 1)
     carry, token = (), ()
-    halo_k, halo_v = [], []
+    if direct:
+        near = memory.reshape(-1, BLOCK, memory.shape[-1])
+        table, loc, most = plan(block_ids, everyone, heads, blocks_here)
+        most = most_of_all(jnp.broadcast_to(most[:, None], (tok_count, 128)))
+        hot = jnp.argmax(most).astype(jnp.int32)
+        overflow = jnp.any((most > BASE) & (jnp.arange(tok_count) != hot))
+        one, three, side = pack(
+            table, near, [(1, 0, BASE), (3, 0, BASE), (0, 0, 16)], (tail,)
+        )
+        two, *more = pack(
+            table, near, [(2, 0, BASE)] + [(k, BASE, EXTRA) for k in range(1, chips)], (side,)
+        )
+        own_one = chip_shift(one, 1)
+        own_three = chip_shift(three, 3)
+        own_two = chip_shift(two, 2)
+        beside = core_swap(side)
+        token = (two,)
     for head in range(heads):
-        carry, dk, dv, token = local_head(
-            head, gates, prev_ok, queries, keys, values, grad_out, hk, hv, carry, token
+        carry, token = local_head(
+            head, gates, prev_ok, queries, keys, values, grad_out, halo, carry, token
         )
         token = (token,)
-        halo_k.append(dk)
-        halo_v.append(dv)
-    ink = passed_along(jnp.concatenate(halo_k, axis=1), "tok", -1)
-    inv = passed_along(jnp.concatenate(halo_v, axis=1), "tok", -1)
-    return tuple(
-        memory_heads(loc, gates, queries, grad_out, carry, ink, inv, returned, returned, returned)
+        if direct and head == 3:
+            token = token + (beside,)
+
+    def finish(where, sources, back):
+        return tuple(memory_heads(where, gates, queries, grad_out, carry, back, sources))
+
+    def full_exchange(back):
+        returned, where = exchange_all(memory, block_ids)
+        return finish(where, [returned], back)
+
+    if not direct:
+        return full_exchange(passed_along(carry[6], "tok", -1))
+
+    def from_device(source):
+        def send(more, one, two, three, halo_grads):
+            late = [chip_shift(more[k - 1], k, source) for k in range(1, chips)]
+            back = passed_along(halo_grads, "tok", -1)
+            passed = [core_swap(block) for block in (one, two, three)]
+            late = summed(late, (back, *passed))
+            return late + core_swap(late), back, *passed
+        return send
+
+    late, back, pass_one, pass_two, pass_three = lax.switch(
+        hot, [from_device(source) for source in range(tok_count)],
+        more, own_one, own_two, own_three, carry[6],
+    )
+    sources = [near, beside, own_one, pass_one, own_two, pass_two, own_three, pass_three, late]
+    return lax.cond(
+        overflow, lambda: full_exchange(back), lambda: finish(loc, sources, back)
     )
 
 

time: 377 us -> 241 us (0.64)
  the two profiles are of different devices: /device:TPU:11 before, /device:TPU:0 now
where the time goes in v2:
time: 241 us; the launch traced here: 239 us
  Pallas kernels  106 us (44%)
  waiting for transfers between devices  95.7 us (40%)
  starting transfers between devices  22.1 us (9%)
  other arithmetic  6.36 us (3%)
  local copies, waits for them, and re-layouts  4.89 us (2%)
  between operations  2.42 us (1%)
    ppermute x6, waiting for transfers between devices, chip_shift(): return lax.ppermute(block, 'tok', route)  83.7 us
    pallas_call x8, Pallas kernels, local_head(): pl.pallas_call(functools.partial(local_kernel, head, len(extra)), grid=(1...  63.4 us
    pallas_call x1, Pallas kernels, memory_heads(): pl.pallas_call(functools.partial(memory_kernel, len(sources)), grid=(head...  28.6 us
    pallas_call x2, Pallas kernels, pack(): pl.pallas_call(functools.partial(pack_kernel, lists, len(after)), out_sha...  8.81 us
    ppermute x6, starting transfers between devices, chip_shift(): return lax.ppermute(block, 'tok', route)  6.65 us
    all_to_all x1, starting transfers between devices, per_device(): lax.all_to_all(jnp.broadcast_to(block_ids[None], (tok_count,) + block_ids...  6.33 us
    ppermute x2, waiting for transfers between devices, most_of_all(): other = lax.ppermute(most, 'mem', [(i, i ^ step) for i in range(count)])  5.5 us
  transfers between devices with their start and end apart: 16, of which 7 were waited for; matrix products, arithmetic and copies ran while one was open for 3% of the time, Pallas kernels for 30%

profile of v2, /device:TPU:0, one launch (start us, length us, event | category | flops | bytes accessed | tf_op | source)
XLA Modules:
  0.0 238.6 jit_solution(7478692393366440691)
XLA Ops:
  0.6 1.3 broadcast_in_dim.129
  1.9 6.3 %all-to-all-start.2 = ((s32[8,2,8,4]{2,3,1,0:T(4,128)}), s32[8,2,8,4]{2,3,1,0:T(4,128)S(1)}, u32[]{:S(2)}, u32[]{:S(2)}) async-start(s32[8,2,8,4]{2,3,1,0:T(4,128)} %broadcast_in_dim.129), calls=%async_computation.2 | async-start | bytes 65536 | tf_op jit(solution)/shard_map/all_to_all | solution.py:412
  8.3 0.8 copy.101
  9.1 0.7 add_divide_fusion.gates
  9.8 4.2 %all-to-all-done.2 = s32[8,2,8,4]{2,3,1,0:T(4,128)S(1)} async-done(((s32[8,2,8,4]{2,3,1,0:T(4,128)}), s32[8,2,8,4]{2,3,1,0:T(4,128)S(1)}, u32[]{:S(2)}, u32[]{:S(2)}) %all-to-all-start.2) | async-done | bytes 2080 | tf_op jit(solution)/shard_map/all_to_all | solution.py:412
  14.0 0.1 fusion.36
  14.1 0.1 copy.99
  14.2 0.1 copy.100
  14.2 0.8 copy.104.after_ref
  15.0 3.0 %tails.1.rest_0_ = bf16[1024,1024]{1,0:T(8,128)(2,1)} custom-call(bf16[1024,1024]{1,0:T(8,128)(2,1)} %k_ref.17, bf16[1024,1024]{1,0:T(8,128)(2,1)} %v_ref.17, s32[8,2,8,4]{3,2,1,0:T(8,128)} %copy.104.after_ref), custom_call_target="tpu_custom_call" | custom-call | tf_op jit(solution)/shard_map/tails/pallas_call | solution.py:311
  18.0 2.9 %collective-permute-start.66 = (bf16[1024,1024]{1,0:T(8,128)(2,1)}, bf16[1024,1024]{1,0:T(8,128)(2,1)}, u32[]{:S(2)}, u32[]{:S(2)}) collective-permute-start(bf16[1024,1024]{1,0:T(8,128)(2,1)} %tails.1.rest_0_), channel_id=1, source_target_pairs={{0,1},{1,2},{2,3},{3,4},{4,5},{5,6},{6,7},{8,9},{9,10},{10,11},{11... | collective-permute-start | bytes 6291464 | tf_op jit(solution)/shard_map/ppermute | solution.py:27
  21.0 0.6 fusion.24
  21.6 0.1 reduce_or.28
  21.6 0.2 fusion.29
  21.8 0.1 fusion.25
  22.0 0.1 select_reduce_fusion.1
  22.1 0.6 broadcast_add_fusion.table
  22.7 4.6 %pack.2 = (bf16[22,128,256]{2,1,0:T(8,128)(2,1)}, bf16[22,128,256]{2,1,0:T(8,128)(2,1)}, bf16[16,128,256]{2,1,0:T(8,128)(2,1)}) custom-call(s32[4,32]{1,0:T(4,128)} %broadcast_add_fusion.table, bf16[128,128,256]{2,1,0:T(8,128)(2,1)} %bitcast.88, bf16[1024,1024]{1,0:T(8,128)(2,1)} %tails.1.rest_0_), custom_call_target="tpu_custom_call" | custom-call | bytes 7864320 | tf_op jit(solution)/shard_map/pack/pallas_call | solution.py:287
  27.3 0.0 copy-start.1
  27.3 4.3 %pack.3 = (bf16[22,128,256]{2,1,0:T(8,128)(2,1)}, bf16[10,128,256]{2,1,0:T(8,128)(2,1)}, bf16[10,128,256]{2,1,0:T(8,128)(2,1)}, bf16[10,128,256]{2,1,0:T(8,128)(2,1)}) custom-call(s32[4,32]{1,0:T(4,128)} %broadcast_add_fusion.table, bf16[128,128,256]{2,1,0:T(8,128)(2,1)} %bitcast.89, bf16[16,128,256]{2,1,0:T(8,128)(2,1)} %get-tuple-element.516.rest_0_), custom_call_target="tpu_custom_call" | custom-call | bytes 6815744 | tf_op jit(solution)/shard_map/pack/pallas_call | solution.py:287
  31.6 0.1 collective-permute-start.67
  31.6 0.1 collective-permute-start.69
  31.7 0.6 collective-permute-start.68
  32.3 0.1 convert_reduce_fusion.1
  32.5 1.3 collective-permute-start.64
  33.8 0.1 dynamic_slice.27
  33.9 0.1 fusion.26
  34.0 2.8 %collective-permute-done.64 = s32[8,128]{0,1:T(8,128)S(1)} collective-permute-done((s32[8,128]{0,1:T(8,128)S(1)}, s32[8,128]{0,1:T(8,128)S(1)}, u32[]{:S(2)}, u32[]{:S(2)}) %collective-permute-start.64) | collective-permute-done | bytes 4128 | tf_op jit(solution)/shard_map/ppermute | solution.py:397
  36.8 1.6 collective-permute-start.65
  38.4 2.7 %collective-permute-done.65 = s32[8,128]{0,1:T(8,128)S(1)} collective-permute-done((s32[8,128]{0,1:T(8,128)S(1)}, s32[8,128]{0,1:T(8,128)S(1)}, u32[]{:S(2)}, u32[]{:S(2)}) %collective-permute-start.65) | collective-permute-done | bytes 4128 | tf_op jit(solution)/shard_map/ppermute | solution.py:397
  41.1 3.3 %collective-permute-start.70 = (bf16[22,128,256]{2,1,0:T(8,128)(2,1)}, bf16[22,128,256]{2,1,0:T(8,128)(2,1)}, u32[]{:S(2)}, u32[]{:S(2)}) collective-permute-start(bf16[22,128,256]{2,1,0:T(8,128)(2,1)} %get-tuple-element.583), channel_id=1, source_target_pairs={{0,6},{1,7},{2,0},{3,1},{4,2},{5,3},{6,4},{7,5},{8,14},{9,15},{10,... | collective-permute-start | bytes 4325384 | tf_op jit(solution)/shard_map/ppermute | solution.py:386
  44.5 1.1 iota_reduce_fusion
  46.3 1.3 and_reduce_fusion
  48.2 7.8 %local_head.8 = (f32[1024,1024]{1,0:T(8,128)S(1)}, f32[1024,1024]{1,0:T(8,128)}, bf16[1024,1024]{1,0:T(8,128)(2,1)}, bf16[1024,1024]{1,0:T(8,128)(2,1)}, f32[512...) custom-call(f32[8]{0:T(128)S(1)} %add_divide_fusion.gates, ...), custom_call_target="tpu_custom_call" | custom-call | flops 8999999488 | bytes 4194304 | tf_op jit(solution)/shard_map/local_head/pallas_call | solution.py:115
  56.0 7.8 %local_head.9 = (f32[1024,1024]{1,0:T(8,128)S(1)}, f32[1024,1024]{1,0:T(8,128)}, bf16[1024,1024]{1,0:T(8,128)(2,1)}, bf16[1024,1024]{1,0:T(8,128)(2,1)}, f32[512...) custom-call(f32[8]{0:T(128)S(1)} %add_divide_fusion.gates, ...), custom_call_target="tpu_custom_call", output_to_operand_aliasing={{0}: (7, {}), {1}: (8, {}), {2}: (9, {}), {3}: (10, {}), {4... | custom-call | flops 8999999488 | bytes 4194304 | tf_op jit(solution)/shard_map/local_head/pallas_call | solution.py:115
  63.8 8.0 %local_head.10 = (f32[1024,1024]{1,0:T(8,128)S(1)}, f32[1024,1024]{1,0:T(8,128)}, bf16[1024,1024]{1,0:T(8,128)(2,1)}, bf16[1024,1024]{1,0:T(8,128)(2,1)}, f32[51...) custom-call(f32[8]{0:T(128)S(1)} %add_divide_fusion.gates, ...), custom_call_target="tpu_custom_call", output_to_operand_aliasing={{0}: (7, {}), {1}: (8, {}), {2}: (9, {}), {3}: (10, {}), {4... | custom-call | flops 8999999488 | bytes 4194304 | tf_op jit(solution)/shard_map/local_head/pallas_call | solution.py:115
  71.7 7.8 %local_head.11 = (f32[1024,1024]{1,0:T(8,128)S(1)}, f32[1024,1024]{1,0:T(8,128)}, bf16[1024,1024]{1,0:T(8,128)(2,1)}, bf16[1024,1024]{1,0:T(8,128)(2,1)}, f32[51...) custom-call(f32[8]{0:T(128)S(1)} %add_divide_fusion.gates, ...), custom_call_target="tpu_custom_call", output_to_operand_aliasing={{0}: (7, {}), {1}: (8, {}), {2}: (9, {}), {3}: (10, {}), {4... | custom-call | flops 8999999488 | bytes 4194304 | tf_op jit(solution)/shard_map/local_head/pallas_call | solution.py:115
  79.5 8.6 %local_head.12 = (f32[1024,1024]{1,0:T(8,128)S(1)}, f32[1024,1024]{1,0:T(8,128)}, bf16[1024,1024]{1,0:T(8,128)(2,1)}, bf16[1024,1024]{1,0:T(8,128)(2,1)}, f32[51...) custom-call(f32[8]{0:T(128)S(1)} %add_divide_fusion.gates, ...), custom_call_target="tpu_custom_call", output_to_operand_aliasing={{0}: (7, {}), {1}: (8, {}), {2}: (9, {}), {3}: (10, {}), {4... | custom-call | flops 8999999488 | bytes 4194304 | tf_op jit(solution)/shard_map/local_head/pallas_call | solution.py:115
  88.1 7.8 %local_head.13 = (f32[1024,1024]{1,0:T(8,128)S(1)}, f32[1024,1024]{1,0:T(8,128)}, bf16[1024,1024]{1,0:T(8,128)(2,1)}, bf16[1024,1024]{1,0:T(8,128)(2,1)}, f32[51...) custom-call(f32[8]{0:T(128)S(1)} %add_divide_fusion.gates, ...), custom_call_target="tpu_custom_call", output_to_operand_aliasing={{0}: (7, {}), {1}: (8, {}), {2}: (9, {}), {3}: (10, {}), {4... | custom-call | flops 8999999488 | bytes 4194304 | tf_op jit(solution)/shard_map/local_head/pallas_call | solution.py:115
  95.9 7.8 %local_head.14 = (f32[1024,1024]{1,0:T(8,128)S(1)}, f32[1024,1024]{1,0:T(8,128)}, bf16[1024,1024]{1,0:T(8,128)(2,1)}, bf16[1024,1024]{1,0:T(8,128)(2,1)}, f32[51...) custom-call(f32[8]{0:T(128)S(1)} %add_divide_fusion.gates, ...), custom_call_target="tpu_custom_call", output_to_operand_aliasing={{0}: (7, {}), {1}: (8, {}), {2}: (9, {}), {3}: (10, {}), {4... | custom-call | flops 8999999488 | bytes 4194304 | tf_op jit(solution)/shard_map/local_head/pallas_call | solution.py:115
  103.7 8.0 %local_head.15 = (f32[1024,1024]{1,0:T(8,128)S(1)}, f32[1024,1024]{1,0:T(8,128)}, bf16[1024,1024]{1,0:T(8,128)(2,1)}, bf16[1024,1024]{1,0:T(8,128)(2,1)}, f32[51...) custom-call(f32[8]{0:T(128)S(1)} %add_divide_fusion.gates, ...), custom_call_target="tpu_custom_call", output_to_operand_aliasing={{0}: (7, {}), {1}: (8, {}), {2}: (9, {}), {3}: (10, {}), {4... | custom-call | flops 8999999488 | bytes 4194304 | tf_op jit(solution)/shard_map/local_head/pallas_call | solution.py:115
  111.7 17.0 %collective-permute-done.69 = bf16[22,128,256]{2,1,0:T(8,128)(2,1)} collective-permute-done((bf16[22,128,256]{2,1,0:T(8,128)(2,1)}, bf16[22,128,256]{2,1,0:T(8,128)(2,1)}, u32[]{:S(2)}, u32[]{:S(2)}) %collective-permute-start.69) | collective-permute-done | bytes 1441824 | tf_op jit(solution)/shard_map/ppermute | solution.py:386
  128.7 7.5 %collective-permute-done.70 = bf16[22,128,256]{2,1,0:T(8,128)(2,1)} collective-permute-done((bf16[22,128,256]{2,1,0:T(8,128)(2,1)}, bf16[22,128,256]{2,1,0:T(8,128)(2,1)}, u32[]{:S(2)}, u32[]{:S(2)}) %collective-permute-start.70) | collective-permute-done | bytes 1441824 | tf_op jit(solution)/shard_map/ppermute | solution.py:386
  136.2 72.2 %conditional.2 = (bf16[10,128,256]{2,1,0:T(8,128)(2,1)S(1)}, bf16[1024,1024]{1,0:T(8,128)(2,1)}, bf16[22,128,256]{2,1,0:T(8,128)(2,1)}, bf16[22,128,256]{2,1,0:T(8,128)(2,1)}, bf16[22,128,256]{2,1,0:T(8,128)(2,1)}) conditional(s32[]{:T(128)} %clamp.21, (bf16[10,128,256]{2,1,0:T(8,128)(2,1)S(1)}, ...), branch_computations={%region_7.8_spmd, %region_8.9_spmd, %region_9.10_spmd, %region_10.... | conditional | flops 327680 | bytes 46006716 | solution.py:463
  136.2 1.3 collective-permute-start.19
  137.5 0.7 collective-permute-start.16
  138.2 1.4 collective-permute-start.20
  139.6 0.1 collective-permute-start.21
  139.7 0.4 collective-permute-start.22
  140.1 0.7 collective-permute-start.17
  140.8 1.3 collective-permute-start.18
  142.1 59.2 %collective-permute-done.18.refs_2_ = bf16[10,128,256]{2,1,0:T(8,128)(2,1)S(1)} collective-permute-done((bf16[10,128,256]{2,1,0:T(8,128)(2,1)}, bf16[10,128,256]{2,1,0:T(8,128)(2,1)S(1)}, u32[]{:S(2)}, u32[]{:S(2)}) %collective-permute-start.18) | collective-permute-done | bytes 655392 | tf_op jit(solution)/shard_map/cond/branch_2_fun/ppermute | solution.py:386
  201.4 0.8 copy-done.20
  202.2 2.4 %summed.10 = bf16[10,128,256]{2,1,0:T(8,128)(2,1)} custom-call(bf16[10,128,256]{2,1,0:T(8,128)(2,1)} %copy-done.5, bf16[10,128,256]{2,1,0:T(8,128)(2,1)} %copy-done.13, bf16[10,128,256]{2,1,0:T(8,128)(2,1)} %copy-done.20, bf16[1024,1024]{1,0:T(8,128)(2,1)} %collective-permute-done.19.refs_3_, bf16[22,128,256]{2,1,0:T(8,128)(2,1)} %collective-permute-done.20.refs_4_, ...), custom_call_target="tpu_custom_call" | custom-call | tf_op jit(solution)/shard_map/cond/branch_2_fun/summed/pallas_call | solution.py:331
  204.6 2.3 collective-permute-done.23
  206.9 1.2 add.212
  208.5 29.9 %conditional.3 = ((bf16[1024,1024]{1,0:T(8,128)(2,1)}, bf16[1024,1024]{1,0:T(8,128)(2,1)}, bf16[1024,1024]{1,0:T(8,128)(2,1)}, bf16[1024,1024]{1,0:T(8,128)(2,1)})) conditional(s32[]{:T(128)} %convert_element_type.39, (s32[2,8,4]{1,2,0:T(4,128)S(1)}, s32[2,8,4]{2,1,0:T(8,128)S(1)}, pred[2,8,4]{2,1,0:T(8,128)(4,1)S(1)}, s32[2,8,4]{2,1,0:T(8,128)S(1)}, ...), branch_computations={%region_15.17_spmd, %region_17.20_spmd} | conditional | flops 4295173632 | bytes 67134248 | solution.py:468
  208.5 0.1 fusion.7
  208.6 0.1 copy.105
  208.7 0.1 fusion.3
  208.8 0.1 eq.104
  208.9 0.2 select_reduce_fusion
  209.1 0.7 reshape.414.loc
  209.8 28.6 %memory_heads.2 = (bf16[1024,1024]{1,0:T(8,128)(2,1)}, bf16[1024,1024]{1,0:T(8,128)(2,1)}, bf16[1024,1024]{1,0:T(8,128)(2,1)}, bf16[1024,1024]{1,0:T(8,128)(2,1)}) custom-call(s32[2,8,4]{2,1,0:T(8,128)} %reshape.414.loc, f32[8]{0:T(128)S(1)} %get-tuple-element.404.gates, ...), custom_call_target="tpu_custom_call", output_to_operand_aliasing={{2}: (9, {}), {3}: (10, {})} | custom-call | flops 4294967296 | bytes 25165824 | tf_op jit(solution)/shard_map/cond/branch_0_fun/memory_heads/pallas_call | solution.py:215
  (48 shorter events, 0.3 us)
Async XLA Ops:
  1.9 12.1 %all-to-all-start.2 = ((s32[8,2,8,4]{2,3,1,0:T(4,128)}), s32[8,2,8,4]{2,3,1,0:T(4,128)S(1)}, u32[]{:S(2)}, u32[]{:S(2)}) async-start(s32[8,2,8,4]{2,3,1,0:T(4,128)} %broadcast_in_dim.129), calls=%async_computation.2 | async-start | bytes 65536 | tf_op jit(solution)/shard_map/all_to_all | solution.py:412
  18.0 30.2 %collective-permute-start.66 = (bf16[1024,1024]{1,0:T(8,128)(2,1)}, bf16[1024,1024]{1,0:T(8,128)(2,1)}, u32[]{:S(2)}, u32[]{:S(2)}) collective-permute-start(bf16[1024,1024]{1,0:T(8,128)(2,1)} %tails.1.rest_0_), channel_id=1, source_target_pairs={{0,1},{1,2},{2,3},{3,4},{4,5},{5,6},{6,7},{8,9},{9,10},{10,11},{11... | collective-permute-start | bytes 6291464 | tf_op jit(solution)/shard_map/ppermute | solution.py:27
  27.3 20.9 %copy-start.1 = (bf16[1024,1024]{1,0:T(8,128)(2,1)S(1)}, bf16[1024,1024]{1,0:T(8,128)(2,1)}, u32[]{:S(2)}) copy-start(bf16[1024,1024]{1,0:T(8,128)(2,1)} %q_ref.15) | copy-start | bytes 6291460
  31.6 48.0 %collective-permute-start.67 = (bf16[16,128,256]{2,1,0:T(8,128)(2,1)}, bf16[16,128,256]{2,1,0:T(8,128)(2,1)S(1)}, u32[]{:S(2)}, u32[]{:S(2)}) collective-permute-start(bf16[16,128,256]{2,1,0:T(8,128)(2,1)} %get-tuple-element.516.rest_0_), channel_id=1, source_target_pairs={{0,1},{1,0},{2,3},{3,2},{4,5},{5,4},{6,7},{7,6},{8,9},{9,8},{10,11... | collective-permute-start | bytes 3145736 | tf_op jit(solution)/shard_map/ppermute | solution.py:390
  31.6 97.1 %collective-permute-start.69 = (bf16[22,128,256]{2,1,0:T(8,128)(2,1)}, bf16[22,128,256]{2,1,0:T(8,128)(2,1)}, u32[]{:S(2)}, u32[]{:S(2)}) collective-permute-start(bf16[22,128,256]{2,1,0:T(8,128)(2,1)} %get-tuple-element.517.rest_0_), channel_id=1, source_target_pairs={{0,4},{1,5},{2,6},{3,7},{4,0},{5,1},{6,2},{7,3},{8,12},{9,13},{10,... | collective-permute-start | bytes 4325384 | tf_op jit(solution)/shard_map/ppermute | solution.py:386
  31.7 97.0 %collective-permute-start.68 = (bf16[22,128,256]{2,1,0:T(8,128)(2,1)}, bf16[22,128,256]{2,1,0:T(8,128)(2,1)}, u32[]{:S(2)}, u32[]{:S(2)}) collective-permute-start(bf16[22,128,256]{2,1,0:T(8,128)(2,1)} %get-tuple-element.582), channel_id=1, source_target_pairs={{0,2},{1,3},{2,4},{3,5},{4,6},{5,7},{6,0},{7,1},{8,10},{9,11},{10,... | collective-permute-start | bytes 4325384 | tf_op jit(solution)/shard_map/ppermute | solution.py:386
  32.5 4.3 %collective-permute-start.64 = (s32[8,128]{0,1:T(8,128)S(1)}, s32[8,128]{0,1:T(8,128)S(1)}, u32[]{:S(2)}, u32[]{:S(2)}) collective-permute-start(s32[8,128]{0,1:T(8,128)S(1)} %broadcast_in_dim.130), channel_id=1, source_target_pairs={{0,8},{8,0},{16,24},{24,16},{1,9},{9,1},{17,25},{25,17},{2,10},{10... | collective-permute-start | bytes 12296 | tf_op jit(solution)/shard_map/ppermute | solution.py:397
  36.8 4.3 %collective-permute-start.65 = (s32[8,128]{0,1:T(8,128)S(1)}, s32[8,128]{0,1:T(8,128)S(1)}, u32[]{:S(2)}, u32[]{:S(2)}) collective-permute-start(s32[8,128]{0,1:T(8,128)S(1)} %broadcast_maximum_fusion), channel_id=1, source_target_pairs={{0,16},{8,24},{16,0},{24,8},{1,17},{9,25},{17,1},{25,9},{2,18},{10... | collective-permute-start | bytes 12296 | tf_op jit(solution)/shard_map/ppermute | solution.py:397
  41.1 95.1 %collective-permute-start.70 = (bf16[22,128,256]{2,1,0:T(8,128)(2,1)}, bf16[22,128,256]{2,1,0:T(8,128)(2,1)}, u32[]{:S(2)}, u32[]{:S(2)}) collective-permute-start(bf16[22,128,256]{2,1,0:T(8,128)(2,1)} %get-tuple-element.583), channel_id=1, source_target_pairs={{0,6},{1,7},{2,0},{3,1},{4,2},{5,3},{6,4},{7,5},{8,14},{9,15},{10,... | collective-permute-start | bytes 4325384 | tf_op jit(solution)/shard_map/ppermute | solution.py:386
  79.5 8.6 %copy-start.2 = (bf16[16,128,256]{2,1,0:T(8,128)(2,1)}, bf16[16,128,256]{2,1,0:T(8,128)(2,1)S(1)}, u32[]{:S(2)}) copy-start(bf16[16,128,256]{2,1,0:T(8,128)(2,1)S(1)} %collective-permute-done.67.rest_8_) | copy-start | bytes 3145732
  103.7 32.5 %copy-start.27 = (bf16[10,128,256]{2,1,0:T(8,128)(2,1)S(1)}, bf16[10,128,256]{2,1,0:T(8,128)(2,1)}, u32[]{:S(2)}) copy-start(bf16[10,128,256]{2,1,0:T(8,128)(2,1)} %get-tuple-element.578) | copy-start | bytes 1966084
  111.7 24.5 %copy-start = (f32[1024,1024]{1,0:T(8,128)}, f32[1024,1024]{1,0:T(8,128)S(1)}, u32[]{:S(2)}) copy-start(f32[1024,1024]{1,0:T(8,128)S(1)} %get-tuple-element.574) | copy-start | bytes 12582916
  136.2 72.3 %copy-start.26 = (s32[2,8,4]{1,2,0:T(4,128)S(1)}, s32[2,8,4]{1,2,0:T(4,128)}, u32[]{:S(2)}) copy-start(s32[2,8,4]{1,2,0:T(4,128)} %param.21) | copy-start | bytes 772
  136.2 65.1 %collective-permute-start.19 = (bf16[1024,1024]{1,0:T(8,128)(2,1)}, bf16[1024,1024]{1,0:T(8,128)(2,1)}, u32[]{:S(2)}, u32[]{:S(2)}) collective-permute-start(bf16[1024,1024]{1,0:T(8,128)(2,1)} %get-tuple-element.342), channel_id=1, source_target_pairs={{1,0},{2,1},{3,2},{4,3},{5,4},{6,5},{7,6},{9,8},{10,9},{11,10},{12... | collective-permute-start | bytes 6291464 | tf_op jit(solution)/shard_map/cond/branch_2_fun/ppermute | solution.py:27
  137.5 2.6 %collective-permute-start.16 = (bf16[10,128,256]{2,1,0:T(8,128)(2,1)S(1)}, bf16[10,128,256]{2,1,0:T(8,128)(2,1)S(1)}, u32[]{:S(2)}, u32[]{:S(2)}) collective-permute-start(bf16[10,128,256]{2,1,0:T(8,128)(2,1)S(1)} %get-tuple-element.339), channel_id=1, source_target_pairs={{2,4},{10,12},{18,20},{26,28}} | collective-permute-start | bytes 1966088 | tf_op jit(solution)/shard_map/cond/branch_2_fun/ppermute | solution.py:386
  138.2 63.1 %collective-permute-start.20 = (bf16[22,128,256]{2,1,0:T(8,128)(2,1)}, bf16[22,128,256]{2,1,0:T(8,128)(2,1)}, u32[]{:S(2)}, u32[]{:S(2)}) collective-permute-start(bf16[22,128,256]{2,1,0:T(8,128)(2,1)} %get-tuple-element.343), channel_id=1, source_target_pairs={{0,1},{1,0},{2,3},{3,2},{4,5},{5,4},{6,7},{7,6},{8,9},{9,8},{10,11... | collective-permute-start | bytes 4325384 | tf_op jit(solution)/shard_map/cond/branch_2_fun/ppermute | solution.py:390
  139.6 61.7 %collective-permute-start.21 = (bf16[22,128,256]{2,1,0:T(8,128)(2,1)}, bf16[22,128,256]{2,1,0:T(8,128)(2,1)}, u32[]{:S(2)}, u32[]{:S(2)}) collective-permute-start(bf16[22,128,256]{2,1,0:T(8,128)(2,1)} %get-tuple-element.344), channel_id=1, source_target_pairs={{0,1},{1,0},{2,3},{3,2},{4,5},{5,4},{6,7},{7,6},{8,9},{9,8},{10,11... | collective-permute-start | bytes 4325384 | tf_op jit(solution)/shard_map/cond/branch_2_fun/ppermute | solution.py:390
  139.7 61.7 %collective-permute-start.22 = (bf16[22,128,256]{2,1,0:T(8,128)(2,1)}, bf16[22,128,256]{2,1,0:T(8,128)(2,1)}, u32[]{:S(2)}, u32[]{:S(2)}) collective-permute-start(bf16[22,128,256]{2,1,0:T(8,128)(2,1)} %get-tuple-element.345), channel_id=1, source_target_pairs={{0,1},{1,0},{2,3},{3,2},{4,5},{5,4},{6,7},{7,6},{8,9},{9,8},{10,11... | collective-permute-start | bytes 4325384 | tf_op jit(solution)/shard_map/cond/branch_2_fun/ppermute | solution.py:390
  140.1 61.2 %copy-start.5 = (bf16[10,128,256]{2,1,0:T(8,128)(2,1)}, bf16[10,128,256]{2,1,0:T(8,128)(2,1)S(1)}, u32[]{:S(2)}) copy-start(bf16[10,128,256]{2,1,0:T(8,128)(2,1)S(1)} %collective-permute-done.16.refs_0_) | copy-start | bytes 1966084 | tf_op jit(solution)/shard_map/cond
  140.1 0.7 collective-permute-start.17
  140.8 60.5 %copy-start.13 = (bf16[10,128,256]{2,1,0:T(8,128)(2,1)}, bf16[10,128,256]{2,1,0:T(8,128)(2,1)S(1)}, u32[]{:S(2)}) copy-start(bf16[10,128,256]{2,1,0:T(8,128)(2,1)S(1)} %collective-permute-done.17.refs_1_) | copy-start | bytes 1966084 | tf_op jit(solution)/shard_map/cond
  140.8 60.5 %collective-permute-start.18 = (bf16[10,128,256]{2,1,0:T(8,128)(2,1)}, bf16[10,128,256]{2,1,0:T(8,128)(2,1)S(1)}, u32[]{:S(2)}, u32[]{:S(2)}) collective-permute-start(bf16[10,128,256]{2,1,0:T(8,128)(2,1)} %get-tuple-element.341), channel_id=1, source_target_pairs={{2,0},{10,8},{18,16},{26,24}} | collective-permute-start | bytes 1966088 | tf_op jit(solution)/shard_map/cond/branch_2_fun/ppermute | solution.py:386
  201.3 0.9 copy-start.20
  204.6 2.3 collective-permute-start.23

commit v3 on v2

--- a/solution.py
+++ b/solution.py
@@ -13,10 +13,11 @@
 R = 4
 HD = 128
 NEG = -1e30
+LOG2E = 1.4426950408889634
 KIND = 512
 VMEM_LIMIT = 56 * 2**20
-BASE = 22
-EXTRA = 10
+MAIN = 18
+SECOND = 7
 ANY = pl.BlockSpec(memory_space=pl.ANY)
 SMEM = pl.BlockSpec(memory_space=pltpu.SMEM)
 
@@ -136,12 +137,12 @@
     return result[:7], result[7]
 
 
-def memory_kernel(n_src, loc, gates, q_ref, g_ref, lo_ref, dqf_ref, dkx_ref, dvx_ref, back_ref,
-                  dk_in, dv_in, *rest):
+def memory_kernel(n_src, n_any, bounds, loc, gates, q_ref, g_ref, lo_ref, dqf_ref, *rest):
     sources = rest[:n_src]
-    out_ref, dq_ref, dk_ref, dv_ref, buf, sems = rest[n_src:]
+    out_ref, dq_ref, token_ref, buf, sems = rest[n_src + n_any:]
+    token_ref[...] = jnp.zeros_like(token_ref)
     head = pl.program_id(0)
-    heads = pl.num_programs(0)
+    start, stop = bounds[0], bounds[1]
     scaling = HD ** -0.5
 
     def fetch(h, slot):
@@ -167,69 +168,94 @@
 
             pick(0, n_src)
 
-    slot = lax.rem(head, 2)
-
-    @pl.when(head == 0)
+    @pl.when((head == 0) & (start < stop))
     def _():
-        fetch(0, 0)
-
-    @pl.when(head + 1 < heads)
+        fetch(start, lax.rem(start, 2))
+
+    @pl.when((head >= start) & (head < stop))
     def _():
-        fetch(head + 1, 1 - slot)
-
+        slot = lax.rem(head, 2)
+
+        @pl.when(head + 1 < stop)
+        def _():
+            fetch(head + 1, 1 - slot)
+
+        for j in range(2 * R):
+            pltpu.make_async_copy(sources[0].at[0], buf.at[slot, j], sems.at[slot, j]).wait()
+        gate = gates[head]
+        for span in range(2):
+            blocks = buf[slot, pl.ds(span * R, R)]
+            mk = blocks[:, :, :HD].reshape(R * BLOCK, HD)
+            mv = blocks[:, :, HD:].reshape(R * BLOCK, HD)
+            rows = pl.ds(span * SPAN, SPAN)
+            q = q_ref[rows, :]
+            gm = (gate * g_ref[rows, :].astype(jnp.float32)).astype(jnp.bfloat16)
+            s = mm(q, mk, ((1,), (1,)))
+            top = jnp.max(s, axis=1, keepdims=True)
+            e = jnp.exp2((s - top) * (scaling * LOG2E))
+            share = 1.0 / jnp.sum(e, axis=1, keepdims=True)
+            mo = mm(e.astype(jnp.bfloat16), mv, ((1,), (0,))) * share
+            dp = mm(gm, mv, ((1,), (1,)))
+            dot = jnp.sum(gm.astype(jnp.float32) * mo, axis=1, keepdims=True)
+            ds = (e * (dp - dot)).astype(jnp.bfloat16)
+            dqm = mm(ds, mk, ((1,), (0,))) * (share * scaling)
+            out_ref[rows, :] = (gate * mo + lo_ref[rows, :]).astype(jnp.bfloat16)
+            dq_ref[rows, :] = (dqm + dqf_ref[rows, :]).astype(jnp.bfloat16)
+
+
+def memory_heads(start, stop, loc, gates, q, g, carry, sources, made, after=()):
+    rows, width = q.shape
+    heads = width // HD
+    bounds = jnp.stack([jnp.int32(start), jnp.int32(stop)])
+
+    def column(h, bounds):
+        return 0, jnp.clip(h, bounds[0], jnp.maximum(bounds[1] - 1, bounds[0]))
+
+    col = pl.BlockSpec((rows, HD), column)
+    full = jax.ShapeDtypeStruct((rows, width), jnp.bfloat16)
+    extra = list(made) + list(after)
+    return pl.pallas_call(
+        functools.partial(memory_kernel, len(sources), len(extra)),
+        grid_spec=pltpu.PrefetchScalarGridSpec(
+            num_scalar_prefetch=1,
+            grid=(heads,),
+            in_specs=[SMEM, SMEM, col, col, col, col] + [ANY] * (len(sources) + len(extra)),
+            out_specs=[col, col, pl.BlockSpec((16, 128), lambda h, bounds: (0, 0))],
+            scratch_shapes=[
+                pltpu.VMEM((2, 2 * R, BLOCK, 2 * HD), jnp.bfloat16),
+                pltpu.SemaphoreType.DMA((2, 2 * R)),
+            ],
+        ),
+        out_shape=[full, full, jax.ShapeDtypeStruct((16, 128), jnp.bfloat16)],
+        input_output_aliases={7 + len(sources) + i: i for i in range(len(made))},
+        compiler_params=pltpu.CompilerParams(vmem_limit_bytes=VMEM_LIMIT),
+        cost_estimate=pl.CostEstimate(flops=14 * 10**9, bytes_accessed=2**20,
+                                      transcendentals=heads * 2 * 512 * 512),
+        name="memory_heads",
+    )(bounds, loc, gates, q, g, carry[0], carry[1], *sources, *extra)
+
+
+def close_kernel(dkx_ref, dvx_ref, back_ref, dk_in, dv_in, after_ref, dk_ref, dv_ref):
     dk_ref[...] = (dkx_ref[...] + back_ref[:SPAN].astype(jnp.float32)).astype(jnp.bfloat16)
     dv_ref[...] = (dvx_ref[...] + back_ref[SPAN:].astype(jnp.float32)).astype(jnp.bfloat16)
-    for j in range(2 * R):
-        pltpu.make_async_copy(sources[0].at[0], buf.at[slot, j], sems.at[slot, j]).wait()
-    gate = gates[head]
-    for span in range(2):
-        blocks = buf[slot, pl.ds(span * R, R)]
-        mk = blocks[:, :, :HD].reshape(R * BLOCK, HD)
-        mv = blocks[:, :, HD:].reshape(R * BLOCK, HD)
-        for half in range(2):
-            rows = pl.ds(span * SPAN + half * HALF, HALF)
-            q = q_ref[rows, :]
-            gm = (gate * g_ref[rows, :].astype(jnp.float32)).astype(jnp.bfloat16)
-            s = mm(q, mk, ((1,), (1,))) * scaling
-            top = jnp.max(s, axis=1, keepdims=True)
-            e = jnp.exp(s - top)
-            total = jnp.sum(e, axis=1, keepdims=True)
-            p = (e * (1.0 / total)).astype(jnp.bfloat16)
-            mo = mm(p, mv, ((1,), (0,)))
-            dp = mm(gm, mv, ((1,), (1,)))
-            dot = jnp.sum(gm.astype(jnp.float32) * mo, axis=1, keepdims=True)
-            ds = (p.astype(jnp.float32) * (dp - dot)).astype(jnp.bfloat16)
-            dqm = mm(ds, mk, ((1,), (0,)))
-            out_ref[rows, :] = (gate * mo + lo_ref[rows, :]).astype(jnp.bfloat16)
-            dq_ref[rows, :] = (scaling * dqm + dqf_ref[rows, :]).astype(jnp.bfloat16)
-
-
-def memory_heads(loc, gates, q, g, carry, back, sources):
-    lo, dqf, dk, dv, dkx, dvx = carry[:6]
-    rows, width = q.shape
-    heads = width // HD
-    col = pl.BlockSpec((rows, HD), lambda h: (0, h))
-    col_half = pl.BlockSpec((SPAN, HD), lambda h: (0, h))
-    lower = pl.BlockSpec((SPAN, HD), lambda h: (1, h))
-    full = jax.ShapeDtypeStruct((rows, width), jnp.bfloat16)
+
+
+def close_grads(carry, back, after):
+    dk, dv, dkx, dvx = carry[2:6]
+    width = dk.shape[1]
+    part = width // 4
+    upper = pl.BlockSpec((SPAN, part), lambda h: (0, h))
+    lower = pl.BlockSpec((SPAN, part), lambda h: (1, h))
     return pl.pallas_call(
-        functools.partial(memory_kernel, len(sources)),
-        grid=(heads,),
-        out_shape=[full] * 4,
-        in_specs=[SMEM, SMEM, col, col, col, col, col_half, col_half, col]
-        + [ANY] * (2 + len(sources)),
-        out_specs=[col, col, lower, lower],
-        scratch_shapes=[
-            pltpu.VMEM((2, 2 * R, BLOCK, 2 * HD), jnp.bfloat16),
-            pltpu.SemaphoreType.DMA((2, 2 * R)),
-        ],
-        input_output_aliases={9: 2, 10: 3},
+        close_kernel,
+        grid=(4,),
+        out_shape=[jax.ShapeDtypeStruct(dk.shape, dk.dtype)] * 2,
+        in_specs=[upper, upper, pl.BlockSpec((2 * SPAN, part), lambda h: (0, h))] + [ANY] * 3,
+        out_specs=[lower, lower],
+        input_output_aliases={3: 0, 4: 1},
         compiler_params=pltpu.CompilerParams(vmem_limit_bytes=VMEM_LIMIT),
-        cost_estimate=pl.CostEstimate(flops=heads * 4 * 2 * 2 * 512 * 512 * 128,
-                                      bytes_accessed=24 * 2**20,
-                                      transcendentals=heads * 2 * 512 * 512),
-        name="memory_heads",
-    )(loc, gates, q, g, lo, dqf, dkx, dvx, back, dk, dv, *sources)
+        name="close_grads",
+    )(dkx, dvx, back, dk, dv, after)
 
 
 def exchange_all(memory, block_ids):
@@ -256,48 +282,69 @@
     return returned.reshape(-1, BLOCK, memory.shape[-1]), loc.astype(jnp.int32)
 
 
-def pack_kernel(lists, n_any, table, near, *rest):
-    outs = rest[n_any:n_any + len(lists)]
+def pack_kernel(groups, n_src, n_any, table, *rest):
+    sources = rest[:n_src]
+    outs = rest[n_src + n_any:n_src + n_any + len(groups)]
     held, sems, sent = rest[-3:]
+    sizes = [sum(count for row, count in group) for group in groups]
     for phase in range(2):
         number = 0
-        for place, (row, start, count) in enumerate(lists):
-            for j in range(count):
-                code = table[row, start + j]
-
-                @pl.when(code >= 0)
-                def _():
-                    copy = pltpu.make_async_copy(near.at[code], held.at[number], sems.at[number])
-                    copy.wait() if phase else copy.start()
-                number += 1
+        for place, group in enumerate(groups):
+            for row, count in group:
+                for j in range(count):
+                    code = table[row, j]
+                    for kind, source in enumerate(sources):
+                        @pl.when((code >= kind * KIND) & (code < (kind + 1) * KIND))
+                        def _():
+                            copy = pltpu.make_async_copy(
+                                source.at[code - kind * KIND], held.at[number], sems.at[number]
+                            )
+                            copy.wait() if phase else copy.start()
+                    number += 1
             if phase:
                 pltpu.make_async_copy(
-                    held.at[pl.ds(number - count, count)], outs[place], sent.at[place]
+                    held.at[pl.ds(number - sizes[place], sizes[place])], outs[place],
+                    sent.at[place],
                 ).start()
     number = 0
-    for place, (row, start, count) in enumerate(lists):
-        pltpu.make_async_copy(
-            held.at[pl.ds(number, count)], outs[place], sent.at[place]
-        ).wait()
-        number += count
-
-
-def pack(table, near, lists, after):
-    total = sum(count for row, start, count in lists)
+    for place, size in enumerate(sizes):
+        pltpu.make_async_copy(held.at[pl.ds(number, size)], outs[place], sent.at[place]).wait()
+        number += size
+
+
+def pack(table, sources, groups, after):
+    sizes = [sum(count for row, count in group) for group in groups]
+    block = sources[0].shape[1:]
+    kind = sources[0].dtype
     return pl.pallas_call(
-        functools.partial(pack_kernel, lists, len(after)),
-        out_shape=[jax.ShapeDtypeStruct((n,) + near.shape[1:], near.dtype) for _, _, n in lists],
-        in_specs=[SMEM, ANY] + [ANY] * len(after),
-        out_specs=[ANY] * len(lists),
+        functools.partial(pack_kernel, groups, len(sources), len(after)),
+        out_shape=[jax.ShapeDtypeStruct((size,) + block, kind) for size in sizes],
+        in_specs=[SMEM] + [ANY] * (len(sources) + len(after)),
+        out_specs=[ANY] * len(groups),
         scratch_shapes=[
-            pltpu.VMEM((total,) + near.shape[1:], near.dtype),
-            pltpu.SemaphoreType.DMA((total,)),
-            pltpu.SemaphoreType.DMA((len(lists),)),
+            pltpu.VMEM((sum(sizes),) + block, kind),
+            pltpu.SemaphoreType.DMA((sum(sizes),)),
+            pltpu.SemaphoreType.DMA((len(groups),)),
         ],
         compiler_params=pltpu.CompilerParams(vmem_limit_bytes=VMEM_LIMIT),
-        cost_estimate=pl.CostEstimate(flops=0, bytes_accessed=total * 2**17, transcendentals=0),
+        cost_estimate=pl.CostEstimate(flops=0, bytes_accessed=2**16, transcendentals=0),
         name="pack",
-    )(table, near, *after)
+    )(table, *sources, *after)
+
+
+def held_back(x, after):
+    def kernel(*refs):
+        pass
+
+    return pl.pallas_call(
+        kernel,
+        out_shape=jax.ShapeDtypeStruct(x.shape, x.dtype),
+        in_specs=[ANY] * (1 + len(after)),
+        out_specs=ANY,
+        input_output_aliases={0: 0},
+        cost_estimate=pl.CostEstimate(flops=0, bytes_accessed=0, transcendentals=0),
+        name="held_back",
+    )(x, *after)
 
 
 def tails(keys, values, after):
@@ -317,25 +364,6 @@
         compiler_params=pltpu.CompilerParams(vmem_limit_bytes=VMEM_LIMIT),
         name="tails",
     )(keys, values, after)
-
-
-def summed(parts, after):
-    def kernel(*refs):
-        total = refs[0][...]
-        for ref in refs[1:len(parts)]:
-            total = total + ref[...]
-        refs[-1][...] = total
-
-    x = parts[0]
-    whole = pl.BlockSpec(memory_space=pltpu.VMEM)
-    return pl.pallas_call(
-        kernel,
-        out_shape=jax.ShapeDtypeStruct(x.shape, x.dtype),
-        in_specs=[whole] * len(parts) + [ANY] * len(after),
-        out_specs=whole,
-        compiler_params=pltpu.CompilerParams(vmem_limit_bytes=VMEM_LIMIT),
-        name="summed",
-    )(*parts, *after)
 
 
 def plan(block_ids, everyone, heads, blocks_here):
@@ -350,8 +378,6 @@
     each = jnp.any(block.reshape(tok_count, -1)[:, :, None] == universe, axis=1)
     need = each.reshape(chips, 2, -1).any(axis=1).reshape(chips, tok_count, shard)
     sibling = lax.dynamic_slice(each, (here ^ 1, here * shard), (1, shard))
-    away = jnp.arange(chips)[:, None] != jnp.arange(tok_count)[None, :] // 2
-    most = jnp.max(jnp.sum(need.astype(jnp.int32), axis=2) * away, axis=0)
     before = jnp.triu(jnp.ones((shard, shard), jnp.bfloat16), 1)
 
     def ranked(wanted):
@@ -359,31 +385,57 @@
         return jnp.where(wanted, rank.astype(jnp.int32), -1)
 
     rank = ranked(need)
-    from_me = lax.dynamic_index_in_dim(rank, here, 1, keepdims=False)
-    sent = jnp.concatenate(
-        [ranked(sibling)]
-        + [lax.dynamic_slice_in_dim(from_me, (chip + k) % chips, 1, 0) for k in range(1, chips)]
-    )
-    slot = jnp.arange(BASE + EXTRA, dtype=jnp.int32)
-    hit = sent[:, None, :] == slot[None, :, None]
-    table = jnp.sum(jnp.where(hit, jnp.arange(1, shard + 1, dtype=jnp.int32), 0), axis=2) - 1
+    left = jnp.maximum(jnp.sum(need.astype(jnp.int32), axis=2) - MAIN, 0)
+    pairs = left.reshape(chips, chips, 2)
+    most = jnp.max(jnp.where(jnp.eye(chips, dtype=bool), 0, pairs.sum(axis=2)))
+    ahead = jnp.stack([jnp.zeros_like(pairs[..., 0]), pairs[..., 0]], axis=2).reshape(left.shape)
+    pooled = jnp.where(rank >= MAIN, rank - MAIN + ahead[:, :, None], -1)
+
+    chip_ids = jnp.arange(chips, dtype=jnp.int32)[:, None]
+
+    def to_others(ranks, device, at_home=-1):
+        mine = lax.dynamic_index_in_dim(ranks, device, 1, keepdims=False)
+        return jnp.where(chip_ids == chip, at_home, mine)
+
+    slot = jnp.arange(MAIN, dtype=jnp.int32)
+    index = jnp.arange(1, shard + 1, dtype=jnp.int32)
+
+    def listed(ranks, slots):
+        hit = ranks[:, None, :] == slots[None, :, None]
+        return jnp.sum(jnp.where(hit, index, 0), axis=2) - 1
+
+    handed = to_others(pooled, here ^ 1)[:, None, :] == 2 * slot[None, :, None] + core
+    from_side = KIND + SECOND * chip_ids + slot
+    own_left = to_others(pooled, here)
+    second = listed(own_left, 2 * slot + core)
+    table = jnp.concatenate([
+        listed(to_others(rank, here, ranked(sibling)), slot),
+        listed(own_left, 2 * slot + 1 - core),
+        jnp.where(jnp.any(handed, axis=2), from_side, second),
+    ])
     sender = jnp.arange(tok_count, dtype=jnp.int32)[:, None]
     got = lax.dynamic_index_in_dim(rank, chip, 0, keepdims=False)
-    away_by = (chip - sender // 2) % chips
-    kind = jnp.where(got < BASE, 2 * away_by + (sender + core) % 2, 2 * chips)
-    place = kind * KIND + jnp.where(got < BASE, got, got - BASE)
+    rest = lax.dynamic_index_in_dim(pooled, chip, 0, keepdims=False)
+    main_place = (1 + (sender + core) % 2) * KIND + MAIN * (sender // 2) + got
+    rest_place = (3 + (rest + core) % 2) * KIND + SECOND * (sender // 2) + rest // 2
+    place = jnp.where(got < MAIN, main_place, rest_place)
     mine = ranked(lax.dynamic_slice(each, (here, (here ^ 1) * shard), (1, shard)))
     place = jnp.where(sender == here, jnp.arange(shard, dtype=jnp.int32), place)
-    place = jnp.where(sender == here ^ 1, KIND + mine, place).reshape(-1)
+    place = jnp.where(sender == here ^ 1, 2 * KIND + MAIN * chip + mine, place).reshape(-1)
     own = (block_ids // blocks_here) * shard + head_of * blocks_here + block_ids % blocks_here
     loc = jnp.sum(jnp.where(own.reshape(-1, 1) == universe, place, 0), axis=1)
-    return table, loc.reshape(block_ids.shape), most
-
-
-def chip_shift(block, distance, only=None):
+    loc = loc.reshape(block_ids.shape)
+    waits = jnp.any(loc >= 3 * KIND, axis=(0, 2))
+    ready = jnp.min(jnp.where(waits, jnp.arange(heads), heads - 1))
+    return table, loc, most, ready
+
+
+def between_chips(block):
     count = lax.axis_size("tok")
-    route = [(i, (i + 2 * distance) % count) for i in range(count) if only in (None, i)]
-    return lax.ppermute(block, "tok", route)
+    groups = [[i for i in range(count) if i % 2 == core] for core in range(2)]
+    return lax.all_to_all(
+        block, "tok", split_axis=0, concat_axis=0, axis_index_groups=groups, tiled=True
+    )
 
 
 def core_swap(block):
@@ -397,7 +449,7 @@
         other = lax.ppermute(most, "mem", [(i, i ^ step) for i in range(count)])
         most = jnp.maximum(most, other)
         step *= 2
-    return most[:, 0]
+    return most
 
 
 def per_device(queries, keys, values, memory, block_ids, gate_bias, grad_out):
@@ -413,61 +465,59 @@
             jnp.broadcast_to(block_ids[None], (tok_count,) + block_ids.shape),
             "tok", split_axis=0, concat_axis=0, tiled=True,
         )
-    tail = tails(keys, values, everyone if direct else block_ids)
+    tail = tails(keys, values, block_ids)
     halo = passed_along(tail, "tok", 1)
     carry, token = (), ()
     if direct:
         near = memory.reshape(-1, BLOCK, memory.shape[-1])
-        table, loc, most = plan(block_ids, everyone, heads, blocks_here)
-        most = most_of_all(jnp.broadcast_to(most[:, None], (tok_count, 128)))
-        hot = jnp.argmax(most).astype(jnp.int32)
-        overflow = jnp.any((most > BASE) & (jnp.arange(tok_count) != hot))
-        one, three, side = pack(
-            table, near, [(1, 0, BASE), (3, 0, BASE), (0, 0, 16)], (tail,)
+        table, loc, most, ready = plan(block_ids, everyone, heads, blocks_here)
+        (main,) = pack(table, [near], [[(chip, MAIN) for chip in range(chips)]], (tail,))
+        own_main = between_chips(main)
+        (side,) = pack(
+            table, [near], [[(chips + chip, SECOND) for chip in range(chips)]], (main,)
         )
-        two, *more = pack(
-            table, near, [(2, 0, BASE)] + [(k, BASE, EXTRA) for k in range(1, chips)], (side,)
-        )
-        own_one = chip_shift(one, 1)
-        own_three = chip_shift(three, 3)
-        own_two = chip_shift(two, 2)
-        beside = core_swap(side)
-        token = (two,)
+        handed = core_swap(side)
+        token = (side,)
     for head in range(heads):
+        if direct and head == 4:
+            token = token + (loc, most)
         carry, token = local_head(
             head, gates, prev_ok, queries, keys, values, grad_out, halo, carry, token
         )
+        if direct and head == 1:
+            most = most_of_all(jnp.broadcast_to(most, (8, 128)) + token.astype(jnp.int32))
+            overflow = most[0, 0] > 2 * SECOND
         token = (token,)
-        if direct and head == 3:
-            token = token + (beside,)
-
-    def finish(where, sources, back):
-        return tuple(memory_heads(where, gates, queries, grad_out, carry, back, sources))
-
-    def full_exchange(back):
+    back = passed_along(carry[6], "tok", -1)
+
+    def finish(start, where, sources, made, after=()):
+        return tuple(memory_heads(
+            start, heads, where, gates, queries, grad_out, carry, sources, made, after
+        )[:2])
+
+    def full_exchange():
         returned, where = exchange_all(memory, block_ids)
-        return finish(where, [returned], back)
+        return finish(0, where, [returned], ())
 
     if not direct:
-        return full_exchange(passed_along(carry[6], "tok", -1))
-
-    def from_device(source):
-        def send(more, one, two, three, halo_grads):
-            late = [chip_shift(more[k - 1], k, source) for k in range(1, chips)]
-            back = passed_along(halo_grads, "tok", -1)
-            passed = [core_swap(block) for block in (one, two, three)]
-            late = summed(late, (back, *passed))
-            return late + core_swap(late), back, *passed
-        return send
-
-    late, back, pass_one, pass_two, pass_three = lax.switch(
-        hot, [from_device(source) for source in range(tok_count)],
-        more, own_one, own_two, own_three, carry[6],
-    )
-    sources = [near, beside, own_one, pass_one, own_two, pass_two, own_three, pass_three, late]
-    return lax.cond(
-        overflow, lambda: full_exchange(back), lambda: finish(loc, sources, back)
-    )
+        return full_exchange() + tuple(close_grads(carry, back, block_ids))
+    (second,) = pack(
+        table, [near, handed],
+        [[(2 * chips + chip, SECOND) for chip in range(chips)]], token,
+    )
+    own_second = between_chips(second)
+    own_main = held_back(own_main, (second,))
+    sources = [near, own_main, core_swap(own_main)]
+    *made, made_token = memory_heads(
+        0, jnp.where(overflow, 0, ready), loc, gates, queries, grad_out, carry, sources, ()
+    )
+    own_second = held_back(own_second, (made_token,))
+    sources += [own_second, core_swap(own_second)]
+    out, dq = lax.cond(
+        overflow, full_exchange, lambda: finish(ready, loc, sources, made)
+    )
+    dk, dv = close_grads(carry, back, out)
+    return out, dq, dk, dv
 
 
 def solution(mesh):

time: 241 us -> 218 us (0.905)
  the two profiles are of different devices: /device:TPU:0 before, /device:TPU:11 now
where the time goes in v3:
time: 218 us; the launch traced here: 214 us
  Pallas kernels  109 us (50%)
  waiting for transfers between devices  60.5 us (28%)
  starting transfers between devices  25.8 us (12%)
  other arithmetic  9.37 us (4%)
  local copies, waits for them, and re-layouts  6.07 us (3%)
  between operations  2.43 us (1%)
    pallas_call x8, Pallas kernels, local_head(): pl.pallas_call(functools.partial(local_kernel, head, len(extra)), grid=(1...  64.1 us
    all_to_all x2, waiting for transfers between devices, between_chips(): lax.all_to_all(block, 'tok', split_axis=0, concat_axis=0, axis_index_grou...  35 us
    pallas_call x2, Pallas kernels, memory_heads(): pl.pallas_call(functools.partial(memory_kernel, len(sources), len(extra))...  24.6 us
    ppermute x2, waiting for transfers between devices, passed_along(): return lax.ppermute(block, axis, route)  21.9 us
    pallas_call x3, Pallas kernels, pack(): pl.pallas_call(functools.partial(pack_kernel, groups, len(sources), len(a...  13 us
    all_to_all x2, starting transfers between devices, between_chips(): lax.all_to_all(block, 'tok', split_axis=0, concat_axis=0, axis_index_grou...  10.7 us
    ppermute x2, starting transfers between devices, passed_along(): return lax.ppermute(block, axis, route)  6.29 us
    all_to_all x1, starting transfers between devices, per_device(): lax.all_to_all(jnp.broadcast_to(block_ids[None], (tok_count,) + block_ids...  5.64 us
  transfers between devices with their start and end apart: 10, of which 5 were waited for; matrix products, arithmetic and copies ran while one was open for 6% of the time, Pallas kernels for 49%

profile of v3, /device:TPU:11, one launch (start us, length us, event | category | flops | bytes accessed | tf_op | source)
XLA Modules:
  0.0 214.0 jit_solution(7265518463784038037)
XLA Ops:
  0.6 1.3 broadcast_in_dim.152
  1.9 5.6 %all-to-all-start.2 = ((s32[8,2,8,4]{2,3,1,0:T(4,128)}), s32[8,2,8,4]{2,3,1,0:T(4,128)S(1)}, u32[]{:S(2)}, u32[]{:S(2)}) async-start(s32[8,2,8,4]{2,3,1,0:T(4,128)} %broadcast_in_dim.152), calls=%async_computation.2 | async-start | bytes 65536 | tf_op jit(solution)/shard_map/all_to_all | solution.py:464
  7.6 1.4 copy.98.after_ref
  8.9 3.0 %tails.1.rest_1_ = bf16[1024,1024]{1,0:T(8,128)(2,1)} custom-call(bf16[1024,1024]{1,0:T(8,128)(2,1)} %k_ref.17, bf16[1024,1024]{1,0:T(8,128)(2,1)} %v_ref.17, s32[2,8,4]{2,1,0:T(8,128)} %copy.98.after_ref), custom_call_target="tpu_custom_call" | custom-call | tf_op jit(solution)/shard_map/tails/pallas_call | solution.py:358
  12.0 3.3 %collective-permute-start = (bf16[1024,1024]{1,0:T(8,128)(2,1)}, bf16[1024,1024]{1,0:T(8,128)(2,1)}, u32[]{:S(2)}, u32[]{:S(2)}) collective-permute-start(bf16[1024,1024]{1,0:T(8,128)(2,1)} %tails.1.rest_1_), channel_id=1, source_target_pairs={{0,1},{1,2},{2,3},{3,4},{4,5},{5,6},{6,7},{8,9},{9,10},{10,11},{11... | collective-permute-start | bytes 6291464 | tf_op jit(solution)/shard_map/ppermute | solution.py:28
  15.5 0.1 copy.104
  15.6 0.1 eq.204
  15.7 0.1 fusion.27
  15.8 0.1 copy.95
  15.9 0.6 fusion.10
  16.6 0.1 convert_reduce_fusion.1
  16.8 0.1 copy.97
  16.9 0.1 copy.100
  17.0 0.2 fusion.15
  17.2 0.1 add_select_fusion.3
  17.3 0.1 broadcast_select_fusion.1
  17.4 0.5 compare_reduce_fusion
  17.8 0.1 copy.103
  18.0 1.1 select_reduce_fusion.2
  19.0 0.1 copy.101
  19.1 0.1 copy.102
  19.2 0.1 copy.99
  19.3 0.1 add_select_fusion.8
  19.4 0.6 pad_add_fusion.1.table
  20.0 5.8 %pack.3.rest_1_ = bf16[72,128,256]{2,1,0:T(8,128)(2,1)} custom-call(s32[12,18]{1,0:T(8,128)} %pad_add_fusion.1.table, bf16[128,128,256]{2,1,0:T(8,128)(2,1)} %bitcast.124, bf16[1024,1024]{1,0:T(8,128)(2,1)} %tails.1.rest_1_), custom_call_target="tpu_custom_call" | custom-call | bytes 65536 | tf_op jit(solution)/shard_map/pack/pallas_call | solution.py:319
  25.8 5.4 %all-to-all-start.3 = ((bf16[72,128,256]{2,1,0:T(8,128)(2,1)}), bf16[72,128,256]{2,1,0:T(8,128)(2,1)}, u32[]{:S(2)}, u32[]{:S(2)}) async-start(bf16[72,128,256]{2,1,0:T(8,128)(2,1)} %pack.3.rest_1_), calls=%async_computation.3 | async-start | bytes 9437184 | tf_op jit(solution)/shard_map/all_to_all | solution.py:436
  31.3 3.6 %pack.4.rest_0_ = bf16[28,128,256]{2,1,0:T(8,128)(2,1)} custom-call(s32[12,18]{1,0:T(8,128)} %pad_add_fusion.1.table, bf16[128,128,256]{2,1,0:T(8,128)(2,1)} %bitcast.125, bf16[72,128,256]{2,1,0:T(8,128)(2,1)} %pack.3.rest_1_), custom_call_target="tpu_custom_call" | custom-call | bytes 65536 | tf_op jit(solution)/shard_map/pack/pallas_call | solution.py:319
  34.8 0.2 fusion.20
  35.0 0.1 fusion.49
  35.1 0.2 select_reduce_fusion
  35.3 0.1 reshape.400.rest_8_.loc
  35.5 0.6 select_reduce_fusion.4
  36.1 9.0 %collective-permute-done.halo_ref = bf16[1024,1024]{1,0:T(8,128)(2,1)} collective-permute-done((bf16[1024,1024]{1,0:T(8,128)(2,1)}, bf16[1024,1024]{1,0:T(8,128)(2,1)}, u32[]{:S(2)}, u32[]{:S(2)}) %collective-permute-start) | collective-permute-done | bytes 2097184 | tf_op jit(solution)/shard_map/ppermute | solution.py:28
  45.1 8.2 %local_head.8 = (f32[1024,1024]{1,0:T(8,128)}, f32[1024,1024]{1,0:T(8,128)}, bf16[1024,1024]{1,0:T(8,128)(2,1)}, bf16[1024,1024]{1,0:T(8,128)(2,1)}, f32[512,102...) custom-call(f32[8]{0:T(128)S(1)} %add_divide_fusion.gates, s32[1]{0:T(128)} %bitcast.9.prev_ok, ...), custom_call_target="tpu_custom_call" | custom-call | flops 8999999488 | bytes 4194304 | tf_op jit(solution)/shard_map/local_head/pallas_call | solution.py:116
  53.3 7.9 %local_head.9 = (f32[1024,1024]{1,0:T(8,128)}, f32[1024,1024]{1,0:T(8,128)}, bf16[1024,1024]{1,0:T(8,128)(2,1)}, bf16[1024,1024]{1,0:T(8,128)(2,1)}, f32[512,102...) custom-call(f32[8]{0:T(128)S(1)} %add_divide_fusion.gates, ...), custom_call_target="tpu_custom_call", output_to_operand_aliasing={{0}: (7, {}), {1}: (8, {}), {2}: (9, {}), {3}: (10, {}), {4... | custom-call | flops 8999999488 | bytes 4194304 | tf_op jit(solution)/shard_map/local_head/pallas_call | solution.py:116
  61.2 1.3 convert_add_fusion
  62.5 0.1 collective-permute-start.1
  62.6 8.1 %local_head.10 = (f32[1024,1024]{1,0:T(8,128)}, f32[1024,1024]{1,0:T(8,128)}, bf16[1024,1024]{1,0:T(8,128)(2,1)}, bf16[1024,1024]{1,0:T(8,128)(2,1)}, f32[512,10...) custom-call(f32[8]{0:T(128)S(1)} %add_divide_fusion.gates, ...), custom_call_target="tpu_custom_call", output_to_operand_aliasing={{0}: (7, {}), {1}: (8, {}), {2}: (9, {}), {3}: (10, {}), {4... | custom-call | flops 8999999488 | bytes 4194304 | tf_op jit(solution)/shard_map/local_head/pallas_call | solution.py:116
  70.7 0.6 fusion.71
  71.3 1.3 collective-permute-start.2
  72.6 7.9 %local_head.11 = (f32[1024,1024]{1,0:T(8,128)}, f32[1024,1024]{1,0:T(8,128)}, bf16[1024,1024]{1,0:T(8,128)(2,1)}, bf16[1024,1024]{1,0:T(8,128)(2,1)}, f32[512,10...) custom-call(f32[8]{0:T(128)S(1)} %add_divide_fusion.gates, ...), custom_call_target="tpu_custom_call", output_to_operand_aliasing={{0}: (7, {}), {1}: (8, {}), {2}: (9, {}), {3}: (10, {}), {4... | custom-call | flops 8999999488 | bytes 4194304 | tf_op jit(solution)/shard_map/local_head/pallas_call | solution.py:116
  80.5 0.6 max.20.rest_9_
  81.1 8.3 %local_head.12 = (f32[1024,1024]{1,0:T(8,128)}, f32[1024,1024]{1,0:T(8,128)}, bf16[1024,1024]{1,0:T(8,128)(2,1)}, bf16[1024,1024]{1,0:T(8,128)(2,1)}, f32[512,10...) custom-call(f32[8]{0:T(128)S(1)} %add_divide_fusion.gates, ...), custom_call_target="tpu_custom_call", output_to_operand_aliasing={{0}: (7, {}), {1}: (8, {}), {2}: (9, {}), {3}: (10, {}), {4... | custom-call | flops 8999999488 | bytes 4194304 | tf_op jit(solution)/shard_map/local_head/pallas_call | solution.py:116
  89.4 7.9 %local_head.13 = (f32[1024,1024]{1,0:T(8,128)}, f32[1024,1024]{1,0:T(8,128)}, bf16[1024,1024]{1,0:T(8,128)(2,1)}, bf16[1024,1024]{1,0:T(8,128)(2,1)}, f32[512,10...) custom-call(f32[8]{0:T(128)S(1)} %add_divide_fusion.gates, ...), custom_call_target="tpu_custom_call", output_to_operand_aliasing={{0}: (7, {}), {1}: (8, {}), {2}: (9, {}), {3}: (10, {}), {4... | custom-call | flops 8999999488 | bytes 4194304 | tf_op jit(solution)/shard_map/local_head/pallas_call | solution.py:116
  97.3 7.9 %local_head.14 = (f32[1024,1024]{1,0:T(8,128)}, f32[1024,1024]{1,0:T(8,128)}, bf16[1024,1024]{1,0:T(8,128)(2,1)}, bf16[1024,1024]{1,0:T(8,128)(2,1)}, f32[512,10...) custom-call(f32[8]{0:T(128)S(1)} %add_divide_fusion.gates, ...), custom_call_target="tpu_custom_call", output_to_operand_aliasing={{0}: (7, {}), {1}: (8, {}), {2}: (9, {}), {3}: (10, {}), {4... | custom-call | flops 8999999488 | bytes 4194304 | tf_op jit(solution)/shard_map/local_head/pallas_call | solution.py:116
  105.1 8.0 %local_head.15 = (f32[1024,1024]{1,0:T(8,128)}, f32[1024,1024]{1,0:T(8,128)}, bf16[1024,1024]{1,0:T(8,128)(2,1)}, bf16[1024,1024]{1,0:T(8,128)(2,1)}, f32[512,10...) custom-call(f32[8]{0:T(128)S(1)} %add_divide_fusion.gates, ...), custom_call_target="tpu_custom_call", output_to_operand_aliasing={{0}: (7, {}), {1}: (8, {}), {2}: (9, {}), {3}: (10, {}), {4... | custom-call | flops 8999999488 | bytes 4194304 | tf_op jit(solution)/shard_map/local_head/pallas_call | solution.py:116
  113.2 1.2 copy-done
  114.4 3.6 %pack.5.refs_1_ = bf16[28,128,256]{2,1,0:T(8,128)(2,1)} custom-call(s32[12,18]{1,0:T(8,128)} %pad_add_fusion.1.table, bf16[128,128,256]{2,1,0:T(8,128)(2,1)} %bitcast.126, bf16[28,128,256]{2,1,0:T(8,128)(2,1)} %copy-done, f32[8,128]{1,0:T(8,128)} %get-tuple-element.200.rest_2_), custom_call_target="tpu_custom_call" | custom-call | bytes 65536 | tf_op jit(solution)/shard_map/pack/pallas_call | solution.py:319
  118.0 21.7 %all-to-all-done.3.refs_0_ = bf16[72,128,256]{2,1,0:T(8,128)(2,1)} async-done(((bf16[72,128,256]{2,1,0:T(8,128)(2,1)}), bf16[72,128,256]{2,1,0:T(8,128)(2,1)}, u32[]{:S(2)}, u32[]{:S(2)}) %all-to-all-start.3) | async-done | bytes 4718624 | tf_op jit(solution)/shard_map/all_to_all | solution.py:436
  139.7 5.3 %all-to-all-start.4 = ((bf16[28,128,256]{2,1,0:T(8,128)(2,1)}), bf16[28,128,256]{2,1,0:T(8,128)(2,1)S(1)}, u32[]{:S(2)}, u32[]{:S(2)}) async-start(bf16[28,128,256]{2,1,0:T(8,128)(2,1)} %pack.5.refs_1_), calls=%async_computation.4 | async-start | bytes 3670016 | tf_op jit(solution)/shard_map/all_to_all | solution.py:436
  145.0 0.1 compare_reduce_fusion.1
  145.1 0.7 select_reduce_fusion.5
  145.8 1.2 slice.7
  147.0 3.0 %collective-permute-start.6 = (bf16[1024,1024]{1,0:T(8,128)(2,1)}, bf16[1024,1024]{1,0:T(8,128)(2,1)}, u32[]{:S(2)}, u32[]{:S(2)}) collective-permute-start(bf16[1024,1024]{1,0:T(8,128)(2,1)} %get-tuple-element.208), channel_id=1, source_target_pairs={{1,0},{2,1},{3,2},{4,3},{5,4},{6,5},{7,6},{9,8},{10,9},{11,10},{12... | collective-permute-start | bytes 6291464 | tf_op jit(solution)/shard_map/ppermute | solution.py:28
  151.2 0.6 pad_add_fusion.2.bounds
  151.8 18.6 %memory_heads.5 = (bf16[1024,1024]{1,0:T(8,128)(2,1)}, bf16[1024,1024]{1,0:T(8,128)(2,1)}, bf16[16,128]{1,0:T(8,128)(2,1)}) custom-call(s32[2]{0:T(128)} %pad_add_fusion.2.bounds, s32[2,8,4]{2,1,0:T(8,128)S(1)} %reshape.400.rest_8_.loc, f32[8]{0:T(128)S(1)} %add_divide_fusion.gates, bf16[1024,1024]{1,0:T(8,128)(2,1)} %q_ref.17, bf16[1024,1024]{1,0:T(8,128)(2,1)} %g_ref.17, ...), custom_call_target="tpu_custom_call" | custom-call | flops 14000000000 | bytes 1048576 | tf_op jit(solution)/shard_map/memory_heads/pallas_call | solution.py:217
  170.4 13.4 %all-to-all-done.4.refs_0_ = bf16[28,128,256]{2,1,0:T(8,128)(2,1)S(1)} async-done(((bf16[28,128,256]{2,1,0:T(8,128)(2,1)}), bf16[28,128,256]{2,1,0:T(8,128)(2,1)S(1)}, u32[]{:S(2)}, u32[]{:S(2)}) %all-to-all-start.4) | async-done | bytes 1835040 | tf_op jit(solution)/shard_map/all_to_all | solution.py:436
  183.8 1.7 collective-permute-start.5
  185.5 3.5 %collective-permute-done.5 = bf16[28,128,256]{2,1,0:T(8,128)(2,1)} collective-permute-done((bf16[28,128,256]{2,1,0:T(8,128)(2,1)S(1)}, bf16[28,128,256]{2,1,0:T(8,128)(2,1)}, u32[]{:S(2)}, u32[]{:S(2)}) %collective-permute-start.5) | collective-permute-done | bytes 1835040 | tf_op jit(solution)/shard_map/ppermute | solution.py:442
  189.0 7.3 %conditional.1 = (bf16[1024,1024]{1,0:T(8,128)(2,1)}, bf16[1024,1024]{1,0:T(8,128)(2,1)}) conditional(s32[]{:T(128)} %convert_element_type.45, (s32[]{:T(128)}, s32[2,8,4]{2,1,0:T(8,128)S(1)}, f32[8]{0:T(128)S(1)}, bf16[1024,1024]{1,0:T(8,128)(2,1)}, bf16[1024,1024]{1,0:T(8,128)(2,1)}, /*index=5*/f32[1024,1024]{1,0:T(8,128)}, ...), branch_computations={%region_12.13_spmd, %region_13.16_spmd} | conditional | flops 14000045056 | bytes 51405652 | solution.py:516
  189.0 1.3 pad_add_fusion.bounds
  190.3 6.0 %memory_heads.3 = (bf16[1024,1024]{1,0:T(8,128)(2,1)}, bf16[1024,1024]{1,0:T(8,128)(2,1)}, bf16[16,128]{1,0:T(8,128)(2,1)}) custom-call(s32[2]{0:T(128)} %pad_add_fusion.bounds, s32[2,8,4]{2,1,0:T(8,128)S(1)} %get-tuple-element.43.loc, f32[8]{0:T(128)S(1)} %get-tuple-element.44.gates, ...), custom_call_target="tpu_custom_call", output_to_operand_aliasing={{0}: (12, {}), {1}: (13, {})} | custom-call | flops 14000000000 | bytes 1048576 | tf_op jit(solution)/shard_map/cond/branch_0_fun/memory_heads/pallas_call | solution.py:217
  196.3 12.9 %collective-permute-done.6.back_ref = bf16[1024,1024]{1,0:T(8,128)(2,1)} collective-permute-done((bf16[1024,1024]{1,0:T(8,128)(2,1)}, bf16[1024,1024]{1,0:T(8,128)(2,1)}, u32[]{:S(2)}, u32[]{:S(2)}) %collective-permute-start.6) | collective-permute-done | bytes 2097184 | tf_op jit(solution)/shard_map/ppermute | solution.py:28
  209.2 4.6 %close_grads.1 = (bf16[1024,1024]{1,0:T(8,128)(2,1)}, bf16[1024,1024]{1,0:T(8,128)(2,1)}) custom-call(f32[512,1024]{1,0:T(8,128)} %get-tuple-element.206.dkx_ref, f32[512,1024]{1,0:T(8,128)} %get-tuple-element.207.dvx_ref, bf16[1024,1024]{1,0:T(8,128)(2,1)} %collective-permute-done.6.back_ref, ...), custom_call_target="tpu_custom_call", output_to_operand_aliasing={{0}: (3, {}), {1}: (4, {})} | custom-call | tf_op jit(solution)/shard_map/close_grads/pallas_call | solution.py:249
  (38 shorter events, 0.3 us)
Async XLA Ops:
  1.9 13.8 %all-to-all-start.2 = ((s32[8,2,8,4]{2,3,1,0:T(4,128)}), s32[8,2,8,4]{2,3,1,0:T(4,128)S(1)}, u32[]{:S(2)}, u32[]{:S(2)}) async-start(s32[8,2,8,4]{2,3,1,0:T(4,128)} %broadcast_in_dim.152), calls=%async_computation.2 | async-start | bytes 65536 | tf_op jit(solution)/shard_map/all_to_all | solution.py:464
  8.9 6.5 %copy-start.6 = (f32[8]{0:T(128)S(1)}, f32[8]{0:T(128)}, u32[]{:S(2)}) copy-start(f32[8]{0:T(128)} %param.14) | copy-start | bytes 100
  8.9 6.5 %copy-start.1 = (s32[2,8,4]{1,2,0:T(4,128)S(1)}, s32[2,8,4]{1,2,0:T(4,128)}, u32[]{:S(2)}) copy-start(s32[2,8,4]{1,2,0:T(4,128)} %param.13) | copy-start | bytes 772
  12.0 33.1 %collective-permute-start = (bf16[1024,1024]{1,0:T(8,128)(2,1)}, bf16[1024,1024]{1,0:T(8,128)(2,1)}, u32[]{:S(2)}, u32[]{:S(2)}) collective-permute-start(bf16[1024,1024]{1,0:T(8,128)(2,1)} %tails.1.rest_1_), channel_id=1, source_target_pairs={{0,1},{1,2},{2,3},{3,4},{4,5},{5,6},{6,7},{8,9},{9,10},{10,11},{11... | collective-permute-start | bytes 6291464 | tf_op jit(solution)/shard_map/ppermute | solution.py:28
  25.8 113.9 %all-to-all-start.3 = ((bf16[72,128,256]{2,1,0:T(8,128)(2,1)}), bf16[72,128,256]{2,1,0:T(8,128)(2,1)}, u32[]{:S(2)}, u32[]{:S(2)}) async-start(bf16[72,128,256]{2,1,0:T(8,128)(2,1)} %pack.3.rest_1_), calls=%async_computation.3 | async-start | bytes 9437184 | tf_op jit(solution)/shard_map/all_to_all | solution.py:436
  35.4 77.8 %collective-permute-start.3 = (bf16[28,128,256]{2,1,0:T(8,128)(2,1)}, bf16[28,128,256]{2,1,0:T(8,128)(2,1)S(1)}, u32[]{:S(2)}, u32[]{:S(2)}) collective-permute-start(bf16[28,128,256]{2,1,0:T(8,128)(2,1)} %pack.4.rest_0_), channel_id=1, source_target_pairs={{0,1},{1,0},{2,3},{3,2},{4,5},{5,4},{6,7},{7,6},{8,9},{9,8},{10,11... | collective-permute-start | bytes 5505032 | tf_op jit(solution)/shard_map/ppermute | solution.py:442
  45.1 8.2 %copy-start.3 = (bf16[1024,1024]{1,0:T(8,128)(2,1)S(1)}, bf16[1024,1024]{1,0:T(8,128)(2,1)}, u32[]{:S(2)}) copy-start(bf16[1024,1024]{1,0:T(8,128)(2,1)} %q_ref.17) | copy-start | bytes 6291460
  45.1 8.2 %copy-start.5 = (bf16[1024,1024]{1,0:T(8,128)(2,1)S(1)}, bf16[1024,1024]{1,0:T(8,128)(2,1)}, u32[]{:S(2)}) copy-start(bf16[1024,1024]{1,0:T(8,128)(2,1)} %g_ref.17) | copy-start | bytes 6291460
  62.5 8.2 %collective-permute-start.1 = (s32[8,128]{1,0:T(8,128)S(1)}, s32[8,128]{1,0:T(8,128)S(1)}, u32[]{:S(2)}, u32[]{:S(2)}) collective-permute-start(s32[8,128]{1,0:T(8,128)S(1)} %convert_add_fusion), channel_id=1, source_target_pairs={{0,8},{8,0},{16,24},{24,16},{1,9},{9,1},{17,25},{25,17},{2,10},{10... | collective-permute-start | bytes 12296 | tf_op jit(solution)/shard_map/ppermute | solution.py:449
  62.6 8.1 %copy-start.2 = (f32[8,128]{1,0:T(8,128)S(1)}, f32[8,128]{1,0:T(8,128)}, u32[]{:S(2)}) copy-start(f32[8,128]{1,0:T(8,128)} %get-tuple-element.150.rest_7_) | copy-start | bytes 12292
  71.3 9.2 %collective-permute-start.2 = (s32[8,128]{1,0:T(8,128)S(1)}, s32[8,128]{1,0:T(8,128)S(1)}, u32[]{:S(2)}, u32[]{:S(2)}) collective-permute-start(s32[8,128]{1,0:T(8,128)S(1)} %fusion.71), channel_id=1, source_target_pairs={{0,16},{8,24},{16,0},{24,8},{1,17},{9,25},{17,1},{25,9},{2,18},{10... | collective-permute-start | bytes 12296 | tf_op jit(solution)/shard_map/ppermute | solution.py:449
  113.2 1.2 copy-start
  139.7 12.1 %collective-permute-start.4 = (bf16[72,128,256]{2,1,0:T(8,128)(2,1)}, bf16[72,128,256]{2,1,0:T(8,128)(2,1)}, u32[]{:S(2)}, u32[]{:S(2)}) collective-permute-start(bf16[72,128,256]{2,1,0:T(8,128)(2,1)} %held_back.2.rest_1_), channel_id=1, source_target_pairs={{0,1},{1,0},{2,3},{3,2},{4,5},{5,4},{6,7},{7,6},{8,9},{9,8},{10,11... | collective-permute-start | bytes 14155784 | tf_op jit(solution)/shard_map/ppermute | solution.py:442
  139.7 44.1 %all-to-all-start.4 = ((bf16[28,128,256]{2,1,0:T(8,128)(2,1)}), bf16[28,128,256]{2,1,0:T(8,128)(2,1)S(1)}, u32[]{:S(2)}, u32[]{:S(2)}) async-start(bf16[28,128,256]{2,1,0:T(8,128)(2,1)} %pack.5.refs_1_), calls=%async_computation.4 | async-start | bytes 3670016 | tf_op jit(solution)/shard_map/all_to_all | solution.py:436
  147.0 62.3 %collective-permute-start.6 = (bf16[1024,1024]{1,0:T(8,128)(2,1)}, bf16[1024,1024]{1,0:T(8,128)(2,1)}, u32[]{:S(2)}, u32[]{:S(2)}) collective-permute-start(bf16[1024,1024]{1,0:T(8,128)(2,1)} %get-tuple-element.208), channel_id=1, source_target_pairs={{1,0},{2,1},{3,2},{4,3},{5,4},{6,5},{7,6},{9,8},{10,9},{11,10},{12... | collective-permute-start | bytes 6291464 | tf_op jit(solution)/shard_map/ppermute | solution.py:28
  183.8 5.2 %collective-permute-start.5 = (bf16[28,128,256]{2,1,0:T(8,128)(2,1)S(1)}, bf16[28,128,256]{2,1,0:T(8,128)(2,1)}, u32[]{:S(2)}, u32[]{:S(2)}) collective-permute-start(bf16[28,128,256]{2,1,0:T(8,128)(2,1)S(1)} %held_back.3), channel_id=1, source_target_pairs={{0,1},{1,0},{2,3},{3,2},{4,5},{5,4},{6,7},{7,6},{8,9},{9,8},{10,11... | collective-permute-start | bytes 5505032 | tf_op jit(solution)/shard_map/ppermute | solution.py:442
